TPU v7x, 256 devices: a whole 4x4x8 slice. The times are simulated.
256 devices in a mesh: dp: 128 (over y, x, z), rep: 2 (over core).
Axes of the slice: x: 4, y: 4, z: 8, core: 2. Of those that a mesh axis runs over, the one named last changes fastest.
Arguments:
- dense_feats: bfloat16 [65536, 256], P(('dp', 'rep')), may hold values from -6 to 6
- bottom_weight: bfloat16 [256, 128], replicated, may hold values from -0.375 to 0.375
- top_weight: bfloat16 [479, 1024], replicated, may hold values from -0.25 to 0.25
- out_weight: bfloat16 [1024], replicated, may hold values from -0.1875 to 0.1875
- hot_table: bfloat16 [4096, 128], replicated, may hold values from -1.796875 to 1.796875
- cold_table: bfloat16 [524288, 128], P('dp'), may hold values from -1.796875 to 1.796875
- hot_index: int32 [65536, 13], P(('dp', 'rep')), may hold values from 0 to 4095
- cold_owner: int32 [65536, 13], P(('dp', 'rep')), may hold values from 0 to 127, all different within a row; in each aligned block of 256 rows (0 to 255, 256 to 511, ...) at most 52 rows name the same one
- cold_row: int32 [65536, 13], P(('dp', 'rep')), may hold values from 0 to 4095
- clicks: int32 [65536], P(('dp', 'rep')), may hold values from 0 to 1
Outputs:
- hot_grad: float32 [4096, 128], replicated
- cold_grad: float32 [524288, 128], P('dp')
- top_grad: float32 [479, 1024], replicated
Inputs may be any that keep to these rules, and one draw needn't show every extreme that they name: `cold_owner`: each sample names 13 different owners. Among the samples of one device no owner is named by more than 52 samples, and on some device some owner is named by exactly 52.
All inputs are finite; a program needn't handle non-finite values.
Results may differ from a plain program's by a relative error of at most 0.0061.
Values may be sent and summed in bfloat16 or wider, within the bound.
A program may use at most 64 MiB of HBM per device.

v0:
```python
import jax
import jax.numpy as jnp
import numpy as np
from jax import lax
from jax.experimental import pallas as pl
from jax.experimental.pallas import tpu as pltpu
from jax.sharding import PartitionSpec as P

MESH = pl.DeviceIdType.MESH
NX, NY, NZ = 4, 4, 8
VMEM_LIMIT = 48 * 1024 * 1024
F32 = jnp.float32
BF16 = jnp.bfloat16
CAP = 52
STRIDE = 56


def place():
    me = lax.axis_index("dp")
    core = lax.axis_index("rep")
    z = lax.rem(me, NZ)
    x = lax.rem(lax.div(me, NZ), NX)
    y = lax.div(me, NZ * NX)
    return x, y, z, core


def peer(x, y, z, core):
    return (y * (NX * NZ) + x * NZ + z, core)


def rows_at(start, size):
    return pl.ds(pl.multiple_of(start, 16), size)


def reduce_kernel(in_ref, out_ref, core_buf, half, buf1, sum1, buf2, sum2, buf3, send_sem, recv_sem):
    x, y, z, core = place()
    partner = peer(x, y, z, 1 - core)
    xs = [peer(lax.rem(x + d, NX), y, z, core) for d in range(1, NX)]
    ys = [peer(x, lax.rem(y + d, NY), z, core) for d in range(1, NY)]
    zs = [peer(x, y, lax.rem(z + d, NZ), core) for d in range(1, NZ)]
    barrier = pltpu.get_barrier_semaphore()
    everyone = [partner] + xs + ys + zs
    for other in everyone:
        pl.semaphore_signal(barrier, inc=1, device_id=other, device_id_type=MESH)
    pl.semaphore_wait(barrier, len(everyone))

    count = [0]

    def send(src, dst, device):
        index = count[0]
        count[0] += 1
        copy = pltpu.make_async_remote_copy(
            src_ref=src, dst_ref=dst, send_sem=send_sem.at[index], recv_sem=recv_sem.at[index],
            device_id=device, device_id_type=MESH,
        )
        copy.start()
        return copy

    def finish(copies):
        for copy in copies:
            copy.wait()

    finish([send(in_ref.at[rows_at((1 - core) * 4096, 4096)], core_buf, partner)])

    @pl.loop(0, 16)
    def _(step):
        here = rows_at(step * 256, 256)
        mine = in_ref[rows_at(core * 4096 + step * 256, 256), :]
        half[here, :] = (mine.astype(F32) + core_buf[here, :].astype(F32)).astype(BF16)

    copies = []
    for d in range(1, 4):
        copies.append(send(half.at[rows_at(lax.rem(x + d, NX) * 512, 512)], buf1.at[0, d - 1], xs[d - 1]))
        copies.append(send(half.at[rows_at(2048 + lax.rem(y + d, NY) * 512, 512)], buf1.at[1, d - 1], ys[d - 1]))
    finish(copies)
    for which, own in ((0, x), (1, y)):

        @pl.loop(0, 4)
        def _(step):
            here = rows_at(step * 128, 128)
            total = half[rows_at(which * 2048 + own * 512 + step * 128, 128), :].astype(F32)
            for d in range(3):
                total += buf1[which, d, here, :].astype(F32)
            sum1[which, here, :] = total

    copies = []
    for d in range(1, 4):
        copies.append(send(sum1.at[0, rows_at(lax.rem(y + d, NY) * 128, 128)], buf2.at[0, d - 1], ys[d - 1]))
        copies.append(send(sum1.at[1, rows_at(lax.rem(x + d, NX) * 128, 128)], buf2.at[1, d - 1], xs[d - 1]))
    finish(copies)
    for which, own in ((0, y), (1, x)):
        total = sum1[which, rows_at(own * 128, 128), :]
        for d in range(3):
            total += buf2[which, d]
        sum2[which] = total

    copies = []
    for d in range(1, 8):
        for which in range(2):
            copies.append(send(sum2.at[which, rows_at(lax.rem(z + d, NZ) * 16, 16)], buf3.at[which, d - 1], zs[d - 1]))
    finish(copies)
    first = (x * 512 + y * 128, 2048 + y * 512 + x * 128)
    for which in range(2):
        total = sum2[which, rows_at(z * 16, 16), :]
        for d in range(7):
            total += buf3[which, d]
        out_ref[rows_at(core * 4096 + first[which] + z * 16, 16), :] = total.astype(BF16)

    copies = []
    for d in range(1, 8):
        for which in range(2):
            block = out_ref.at[rows_at(core * 4096 + first[which] + z * 16, 16)]
            copies.append(send(block, block, zs[d - 1]))
    finish(copies)
    copies = []
    for d in range(1, 4):
        block = out_ref.at[rows_at(core * 4096 + first[0], 128)]
        copies.append(send(block, block, ys[d - 1]))
        block = out_ref.at[rows_at(core * 4096 + first[1], 128)]
        copies.append(send(block, block, xs[d - 1]))
    finish(copies)
    copies = []
    for d in range(1, 4):
        block = out_ref.at[rows_at(core * 4096 + x * 512, 512)]
        copies.append(send(block, block, xs[d - 1]))
        block = out_ref.at[rows_at(core * 4096 + 2048 + y * 512, 512)]
        copies.append(send(block, block, ys[d - 1]))
    finish(copies)
    block = out_ref.at[rows_at(core * 4096, 4096)]
    finish([send(block, block, partner)])


def reduce_all(values):
    return pl.pallas_call(
        reduce_kernel,
        out_shape=jax.ShapeDtypeStruct((8192, 128), BF16),
        in_specs=[pl.BlockSpec(memory_space=pltpu.VMEM)],
        out_specs=pl.BlockSpec(memory_space=pltpu.VMEM),
        scratch_shapes=[
            pltpu.VMEM((4096, 128), BF16),
            pltpu.VMEM((4096, 128), BF16),
            pltpu.VMEM((2, 3, 512, 128), BF16),
            pltpu.VMEM((2, 512, 128), F32),
            pltpu.VMEM((2, 3, 128, 128), F32),
            pltpu.VMEM((2, 128, 128), F32),
            pltpu.VMEM((2, 7, 16, 128), F32),
            pltpu.SemaphoreType.DMA((54,)),
            pltpu.SemaphoreType.DMA((54,)),
        ],
        compiler_params=pltpu.CompilerParams(
            collective_id=0, has_side_effects=True, vmem_limit_bytes=VMEM_LIMIT
        ),
        name="reduce_all",
    )(values)


def pair_sum_kernel(in_ref, out_ref, held, got, send_sem, recv_sem):
    x, y, z, core = place()
    partner = peer(x, y, z, 1 - core)
    barrier = pltpu.get_barrier_semaphore()
    pl.semaphore_signal(barrier, inc=1, device_id=partner, device_id_type=MESH)
    pl.semaphore_wait(barrier, 1)
    copies = []
    for part in range(4):
        here = pl.ds(part * 1024, 1024)
        held[here, :] = in_ref[here, :].astype(BF16)
        copy = pltpu.make_async_remote_copy(
            src_ref=held.at[here], dst_ref=got.at[here], send_sem=send_sem.at[part],
            recv_sem=recv_sem.at[part], device_id=partner, device_id_type=MESH,
        )
        copy.start()
        copies.append(copy)
    for part in range(4):
        here = pl.ds(part * 1024, 1024)
        copies[part].wait()
        out_ref[here, :] = held[here, :].astype(F32) + got[here, :].astype(F32)


def pair_sum(values):
    return pl.pallas_call(
        pair_sum_kernel,
        out_shape=jax.ShapeDtypeStruct((4096, 128), F32),
        in_specs=[pl.BlockSpec(memory_space=pltpu.VMEM)],
        out_specs=pl.BlockSpec(memory_space=pltpu.VMEM),
        scratch_shapes=[
            pltpu.VMEM((4096, 128), BF16),
            pltpu.VMEM((4096, 128), BF16),
            pltpu.SemaphoreType.DMA((4,)),
            pltpu.SemaphoreType.DMA((4,)),
        ],
        compiler_params=pltpu.CompilerParams(
            collective_id=1, has_side_effects=True, vmem_limit_bytes=VMEM_LIMIT
        ),
        name="pair_sum",
    )(values)


def params():
    return pltpu.CompilerParams(vmem_limit_bytes=VMEM_LIMIT)


def iota(shape, dimension):
    return lax.broadcasted_iota(jnp.int32, shape, dimension)


def build_kernel(owner_ref, row_ref, query_ref, slot_ref, rank, rows, table):
    x, y, z, _ = place()
    owner = owner_ref[...]
    dz = (lax.bitwise_and(owner, 7) - z + 8) & 7
    dx = (lax.bitwise_and(lax.shift_right_logical(owner, 3), 3) - x + 4) & 3
    dy = (lax.shift_right_logical(owner, 5) - y + 4) & 3
    relative = dz * 16 + dy * 4 + dx
    row = row_ref[...].astype(F32)
    owner = owner.astype(F32)
    lane = iota((256, 128), 1)
    named = jnp.zeros((256, 128), F32)
    wanted = jnp.zeros((256, 128), F32)
    for f in range(13):
        here = relative[:, f : f + 1] == lane
        named = jnp.where(here, 1.0, named)
        wanted = jnp.where(here, row[:, f : f + 1], wanted)
    before = jnp.where(iota((256, 256), 1) < iota((256, 256), 0), 1.0, 0.0).astype(BF16)
    count = jnp.dot(before, named.astype(BF16), preferred_element_type=F32)
    slots = jnp.zeros((256, 128), F32)
    for f in range(13):
        here = relative[:, f : f + 1] == lane
        mine = jnp.sum(jnp.where(here, count, 0.0), axis=1, keepdims=True)
        slots = jnp.where(lane == f, owner[:, f : f + 1] * STRIDE + mine, slots)
    slot_ref[...] = slots.T[0:16, :].astype(jnp.int32)
    rank[...] = jnp.where(named > 0.0, count, -1.0)
    rows[...] = wanted
    table[...] = jnp.zeros((128, 128), F32)

    for p in range(CAP):
        chosen = jnp.where(rank[...] == float(p), rows[...], 0.0)
        table[p : p + 1, :] = jnp.sum(chosen, axis=0, keepdims=True)

    query_ref[...] = table[...].T.astype(jnp.int32).reshape(8, 16, 128)


def build_requests(cold_owner, cold_row):
    return pl.pallas_call(
        build_kernel,
        out_shape=(
            jax.ShapeDtypeStruct((8, 16, 128), jnp.int32),
            jax.ShapeDtypeStruct((16, 256), jnp.int32),
        ),
        scratch_shapes=[pltpu.VMEM((256, 128), F32), pltpu.VMEM((256, 128), F32), pltpu.VMEM((128, 128), F32)],
        compiler_params=params(),
        name="build_requests",
    )(cold_owner, cold_row)


def request_kernel(query_ref, out_ref, middle, turned, send_sem, recv_sem):
    x, y, z, core = place()
    plane = [(dx, dy) for dy in range(4) for dx in range(4)]
    zs = [peer(x, y, lax.rem(z + d, NZ), core) for d in range(1, NZ)]
    xys = [peer(lax.rem(x + dx, NX), lax.rem(y + dy, NY), z, core) for dx, dy in plane[1:]]
    barrier = pltpu.get_barrier_semaphore()
    for other in zs + xys:
        pl.semaphore_signal(barrier, inc=1, device_id=other, device_id_type=MESH)
    pl.semaphore_wait(barrier, len(zs) + len(xys))
    copies = []
    for d in range(1, 8):
        copy = pltpu.make_async_remote_copy(
            src_ref=query_ref.at[d], dst_ref=middle.at[d], send_sem=send_sem.at[d], recv_sem=recv_sem.at[d],
            device_id=zs[d - 1], device_id_type=MESH,
        )
        copy.start()
        copies.append(copy)
    middle[0] = query_ref[0]
    for copy in copies:
        copy.wait()
    for d in range(8):
        for k in range(16):
            turned[k, d : d + 1, :] = middle[d, k : k + 1, :]
    copies = []
    for k in range(1, 16):
        copy = pltpu.make_async_remote_copy(
            src_ref=turned.at[k], dst_ref=out_ref.at[k], send_sem=send_sem.at[7 + k], recv_sem=recv_sem.at[7 + k],
            device_id=xys[k - 1], device_id_type=MESH,
        )
        copy.start()
        copies.append(copy)
    out_ref[0] = turned[0]
    for copy in copies:
        copy.wait()


def exchange_requests(query):
    return pl.pallas_call(
        request_kernel,
        out_shape=jax.ShapeDtypeStruct((16, 8, 128), jnp.int32),
        in_specs=[pl.BlockSpec(memory_space=pltpu.VMEM)],
        out_specs=pl.BlockSpec(memory_space=pltpu.VMEM),
        scratch_shapes=[
            pltpu.VMEM((8, 16, 128), jnp.int32),
            pltpu.VMEM((16, 8, 128), jnp.int32),
            pltpu.SemaphoreType.DMA((23,)),
            pltpu.SemaphoreType.DMA((23,)),
        ],
        compiler_params=pltpu.CompilerParams(collective_id=2, has_side_effects=True, vmem_limit_bytes=VMEM_LIMIT),
        name="exchange_requests",
    )(query)


def source_of(r, x, y, z):
    dz, dx, dy = lax.rem(r, 8), lax.rem(lax.div(r, 8), 4), lax.div(r, 32)
    return lax.rem(y - dy + 4, 4) * 32 + lax.rem(x - dx + 4, 4) * 8 + lax.rem(z - dz + 8, 8)


def widen(wide, ref, rows):
    @pl.loop(0, rows // 256)
    def _(step):
        here = pl.ds(pl.multiple_of(step * 256, 256), 256)
        wide[here, :] = ref[here, :].astype(F32)


def lookup_kernel(want_ref, table_ref, out_ref, wide, tile):
    x, y, z, _ = place()
    widen(wide, table_ref, 4096)

    @pl.loop(0, 128)
    def _(r):
        for p in range(CAP):
            tile[p : p + 1, :] = wide[pl.ds(want_ref[r, p], 1), :]
        out_ref[source_of(r, x, y, z)] = tile[0:CAP, :].astype(BF16)


def lookup_rows(want, table):
    return pl.pallas_call(
        lookup_kernel,
        out_shape=jax.ShapeDtypeStruct((128, CAP, 128), BF16),
        in_specs=[pl.BlockSpec(memory_space=pltpu.SMEM), pl.BlockSpec(memory_space=pltpu.VMEM)],
        out_specs=pl.BlockSpec(memory_space=pltpu.VMEM),
        scratch_shapes=[pltpu.VMEM((4096, 128), F32), pltpu.VMEM((64, 128), F32)],
        compiler_params=params(),
        name="lookup_rows",
    )(want, table)


def near_kernel(index_ref, table_ref, dense_ref, weight_ref, out_ref, bottom_ref, wide, held):
    widen(wide, table_ref, 4096)
    bottom = jnp.maximum(jnp.dot(dense_ref[...], weight_ref[...], preferred_element_type=F32), 0.0)
    bottom_ref[...] = bottom.astype(BF16)
    held[...] = bottom

    @pl.loop(0, 32)
    def _(g):
        out_rows = []
        start = pl.multiple_of(g * 8, 8)
        out_ref[g, 0:16, :] = jnp.concatenate(
            [held[pl.ds(start, 8), :]]
            + [wide[pl.ds(index_ref[0, g * 8 + k], 1), :] for k in range(8)], axis=0
        ).astype(BF16)
        for f in range(1, 13, 2):
            rows = [wide[pl.ds(index_ref[f + k // 8, g * 8 + k % 8], 1), :] for k in range(16)]
            out_ref[g, 8 + f * 8 : 24 + f * 8, :] = jnp.concatenate(rows, axis=0).astype(BF16)


def near_rows(hot_index, hot_table, dense, weight):
    vmem = pl.BlockSpec(memory_space=pltpu.VMEM)
    return pl.pallas_call(
        near_kernel,
        out_shape=(jax.ShapeDtypeStruct((32, 112, 128), BF16), jax.ShapeDtypeStruct((256, 128), BF16)),
        in_specs=[pl.BlockSpec(memory_space=pltpu.SMEM), vmem, vmem, vmem],
        out_specs=(vmem, vmem),
        scratch_shapes=[pltpu.VMEM((4096, 128), F32), pltpu.VMEM((256, 128), F32)],
        compiler_params=params(),
        name="near_rows",
    )(hot_index, hot_table, dense, weight)


def main_kernel(
    slot_ref, got_ref, near_ref, bottom_ref, weight0_ref, weight_ref, out_weight_ref, click_ref,
    sent_ref, hot_ref, low_ref, grad_ref,
    wide, stack, far, pairs, hidden, slope, terms,
):
    @pl.loop(0, 128)
    def _(d):
        wide[pl.ds(pl.multiple_of(d * STRIDE, 8), CAP), :] = got_ref[d].astype(F32)

    far[104:144, :] = jnp.zeros((40, 128), F32)
    same = (iota((256, 256), 0) & 7) == (iota((256, 256), 1) & 7)
    fold = jnp.where((iota((256, 128), 0) >> 3) == (iota((256, 128), 1) & 31), 1.0, 0.0).astype(BF16)
    unfold = jnp.where((iota((128, 256), 1) >> 3) == (iota((128, 256), 0) & 31), 1.0, 0.0).astype(BF16)
    quarter = iota((8, 128), 1) >> 5
    zero8 = jnp.zeros((8, 128), F32)

    @pl.loop(0, 32)
    def _(g):
        for f in range(13):
            for k in range(8):
                far[f * 8 + k : f * 8 + k + 1, :] = wide[pl.ds(slot_ref[f, g * 8 + k], 1), :]
        stack[g, 0:112, :] = near_ref[g]
        stack[g, 112:256, :] = far[...].astype(BF16)
        group = stack[g]
        dots = lax.dot_general(group, group, (((1,), (1,)), ((), ())), preferred_element_type=F32)
        dots = jnp.where(same, dots, 0.0).astype(BF16)
        folded = jnp.dot(dots, fold, preferred_element_type=F32)
        for b in range(7):
            block = zero8
            for q in range(4):
                i = 4 * b + q
                block = jnp.where(quarter == q, folded[i * 8 : i * 8 + 8, :], block)
            pairs[pl.ds(pl.multiple_of(g * 8, 8), 8), b * 128 : b * 128 + 128] = block

    for b in range(7):
        i = 4 * b + (iota((256, 128), 1) >> 5)
        j = iota((256, 128), 1) & 31
        low_ref[:, b * 128 : b * 128 + 128] = jnp.where(i > j, pairs[:, b * 128 : b * 128 + 128], 0.0).astype(BF16)

    total = jnp.zeros((256, 128), F32)
    for n in range(4):
        here = slice(n * 256, n * 256 + 256)
        hidden[:, here] = jnp.dot(bottom_ref[...], weight0_ref[:, here], preferred_element_type=F32) + jnp.dot(
            low_ref[...], weight_ref[:, here], preferred_element_type=F32
        )
    for n in range(8):
        here = slice(n * 128, n * 128 + 128)
        v = hidden[:, here]
        c = 0.7978845608028654
        square = v * v
        t = jnp.tanh(c * v * (1.0 + 0.044715 * square))
        weight = out_weight_ref[:, here].astype(F32)
        act = (0.5 * v * (1.0 + t)).astype(BF16).astype(F32)
        total = total + act * weight
        slope[:, here] = weight * (0.5 * (1.0 + t) + 0.5 * c * v * (1.0 - t * t) * (1.0 + 0.134145 * square))
    logits = jnp.sum(total, axis=1, keepdims=True)
    errors = 1.0 / (1.0 + jnp.exp(-logits)) - click_ref[...].astype(F32)
    grad_ref[...] = (slope[...] * errors).astype(BF16)
    for b in range(7):
        here = slice(b * 128, b * 128 + 128)
        pairs[:, here] = lax.dot_general(
            grad_ref[...], weight_ref[here, :], (((1,), (1,)), ((), ())), preferred_element_type=F32
        )

    @pl.loop(0, 7)
    def _(step):
        wide[pl.ds(pl.multiple_of(step * 1024, 1024), 1024), :] = jnp.zeros((1024, 128), F32)

    @pl.loop(0, 32)
    def _(g):
        rows = []
        for b in range(7):
            block = pairs[pl.ds(pl.multiple_of(g * 8, 8), 8), b * 128 : b * 128 + 128]
            for q in range(4):
                rows.append(jnp.where(quarter == q, block, 0.0))
        rows += [zero8] * 4
        spread = jnp.dot(jnp.concatenate(rows, axis=0).astype(BF16), unfold, preferred_element_type=F32)
        spread = jnp.where(same, spread, 0.0).astype(BF16)
        result = jnp.dot(spread, stack[g], preferred_element_type=F32)
        hot_ref[g] = result[0:128, :].astype(BF16)
        terms[...] = result
        for f in range(13):
            for k in range(8):
                row = 112 + f * 8 + k
                wide[pl.ds(slot_ref[f, g * 8 + k], 1), :] = terms[row : row + 1, :]

    @pl.loop(0, 128)
    def _(d):
        sent_ref[d] = wide[pl.ds(pl.multiple_of(d * STRIDE, 8), CAP), :].astype(BF16)


def main_part(slot, got, near, bottom, weight0, weight, out_weight, clicks):
    vmem = pl.BlockSpec(memory_space=pltpu.VMEM)
    return pl.pallas_call(
        main_kernel,
        out_shape=(
            jax.ShapeDtypeStruct((128, CAP, 128), BF16),
            jax.ShapeDtypeStruct((32, 128, 128), BF16),
            jax.ShapeDtypeStruct((256, 896), BF16),
            jax.ShapeDtypeStruct((256, 1024), BF16),
        ),
        in_specs=[pl.BlockSpec(memory_space=pltpu.SMEM)] + [vmem] * 7,
        out_specs=(vmem,) * 4,
        scratch_shapes=[
            pltpu.VMEM((128 * STRIDE, 128), F32),
            pltpu.VMEM((32, 256, 128), BF16),
            pltpu.VMEM((144, 128), F32),
            pltpu.VMEM((256, 896), F32),
            pltpu.VMEM((256, 1024), F32),
            pltpu.VMEM((256, 1024), F32),
            pltpu.VMEM((256, 128), F32),
        ],
        compiler_params=params(),
        name="main_part",
    )(slot, got, near, bottom, weight0, weight, out_weight, clicks)


def hot_kernel(index_ref, column_ref, value_ref, bottom_ref, low_ref, grad_ref, out_ref, halves, top):
    for g in range(32):
        high = column_ref[:, g : g + 1] >> 11
        value = value_ref[g].astype(F32)
        halves[g * 128 : g * 128 + 128, 0:128] = jnp.where(high == 0, value, 0.0).astype(BF16)
        halves[g * 128 : g * 128 + 128, 128:256] = jnp.where(high == 1, value, 0.0).astype(BF16)

    @pl.loop(0, 8)
    def _(m):
        start = pl.multiple_of(m * 256, 256)
        total = jnp.zeros((256, 256), F32)
        for n in range(4):
            index = jnp.broadcast_to(index_ref[:, n * 1024 : n * 1024 + 1024], (256, 1024)) & 2047
            hits = jnp.where(index == iota((256, 1024), 0) + m * 256, 1.0, 0.0).astype(BF16)
            total = total + jnp.dot(hits, halves[n * 1024 : n * 1024 + 1024, :], preferred_element_type=F32)
        out_ref[pl.ds(start, 256), :] = total[:, 0:128].astype(BF16)
        out_ref[pl.ds(start + 2048, 256), :] = total[:, 128:256].astype(BF16)

    top[472:480, :] = jnp.zeros((8, 1024), F32)
    top[0:128, :] = lax.dot_general(
        bottom_ref[...], grad_ref[...], (((0,), (0,)), ((), ())), preferred_element_type=F32
    )
    for b in range(7):
        part = lax.dot_general(
            low_ref[:, b * 128 : b * 128 + 128], grad_ref[...], (((0,), (0,)), ((), ())), preferred_element_type=F32
        )
        for q in range(4):
            i = 4 * b + q
            if 0 < i < 27:
                at = 128 + i * (i - 1) // 2
                top[at : at + i, :] = part[q * 32 : q * 32 + i, :]
    for n in range(8):
        out_ref[4096 + n * 480 : 4576 + n * 480, :] = top[:, n * 128 : n * 128 + 128].astype(BF16)
    out_ref[7936:8192, :] = jnp.zeros((256, 128), BF16)


def hot_and_top(index, column, value, bottom, low, grad):
    return pl.pallas_call(
        hot_kernel,
        out_shape=jax.ShapeDtypeStruct((8192, 128), BF16),
        scratch_shapes=[pltpu.VMEM((4096, 256), BF16), pltpu.VMEM((480, 1024), F32)],
        compiler_params=params(),
        name="hot_and_top",
    )(index, column, value, bottom, low, grad)


def cold_kernel(index_ref, column_ref, value_ref, out_ref, halves):
    x, y, z, _ = place()
    pad = jnp.zeros((64 - CAP, 128), F32)
    for r in range(128):
        high = column_ref[0:64, r : r + 1] >> 11
        value = jnp.concatenate([value_ref[source_of(r, x, y, z)].astype(F32), pad], axis=0)
        halves[r * 64 : r * 64 + 64, 0:128] = jnp.where(high == 0, value, 0.0).astype(BF16)
        halves[r * 64 : r * 64 + 64, 128:256] = jnp.where(high == 1, value, 0.0).astype(BF16)

    @pl.loop(0, 8)
    def _(m):
        start = pl.multiple_of(m * 256, 256)
        total = jnp.zeros((256, 256), F32)
        for n in range(8):
            index = jnp.broadcast_to(index_ref[:, n * 1024 : n * 1024 + 1024], (256, 1024)) & 2047
            hits = jnp.where(index == iota((256, 1024), 0) + m * 256, 1.0, 0.0).astype(BF16)
            total = total + jnp.dot(hits, halves[n * 1024 : n * 1024 + 1024, :], preferred_element_type=F32)
        out_ref[pl.ds(start, 256), :] = total[:, 0:128]
        out_ref[pl.ds(start + 2048, 256), :] = total[:, 128:256]


def cold_sums(index, column, value):
    return pl.pallas_call(
        cold_kernel,
        out_shape=jax.ShapeDtypeStruct((4096, 128), F32),
        scratch_shapes=[pltpu.VMEM((8192, 256), BF16)],
        compiler_params=params(),
        name="cold_sums",
    )(index, column, value)


def format_kernel(in_ref, hot_ref, top_ref):
    hot_ref[...] = in_ref[0:4096, :].astype(F32)
    for n in range(8):
        top_ref[:, n * 128 : n * 128 + 128] = in_ref[4096 + n * 480 : 4576 + n * 480, :].astype(F32)[0:479, :]


def format_sums(values):
    return pl.pallas_call(
        format_kernel,
        out_shape=(jax.ShapeDtypeStruct((4096, 128), F32), jax.ShapeDtypeStruct((479, 1024), F32)),
        compiler_params=params(),
        name="format_sums",
    )(values)


def weight_rows():
    rows = np.full((896,), 479, np.int32)
    for i in range(27):
        for j in range(27):
            if i != j:
                a, b = max(i, j), min(i, j)
                rows[i * 32 + j] = 128 + a * (a - 1) // 2 + b
    return rows


def body(
    dense_feats,
    bottom_weight,
    top_weight,
    out_weight,
    hot_table,
    cold_table,
    hot_index,
    cold_owner,
    cold_row,
    clicks,
):
    query, slot = build_requests(cold_owner, cold_row)
    wanted = exchange_requests(query).reshape(128, 128)
    found_rows = lookup_rows(wanted, cold_table)
    got = lax.all_to_all(found_rows, "dp", split_axis=0, concat_axis=0, tiled=True)
    hot_fields = hot_index.T
    near, bottom = near_rows(hot_fields, hot_table, dense_feats, bottom_weight)
    weight = jnp.concatenate([top_weight, jnp.zeros((1, 1024), BF16)], axis=0)[weight_rows()]
    outgoing, hot_terms, low, grad = main_part(
        slot, got, near, bottom, top_weight[:128], weight, out_weight.reshape(1, 1024), clicks.reshape(256, 1)
    )
    returned = lax.all_to_all(outgoing, "dp", split_axis=0, concat_axis=0, tiled=True)
    hot_groups = jnp.pad(hot_fields.reshape(13, 32, 8).transpose(1, 0, 2), ((0, 0), (1, 2), (0, 0)), constant_values=-1)
    hot_groups = hot_groups.reshape(32, 128)
    sums = hot_and_top(hot_groups.reshape(1, 4096), hot_groups.T, hot_terms, bottom, low, grad)
    hot_grad, top_grad = format_sums(reduce_all(sums))
    local_cold = cold_sums(wanted[:, :64].reshape(1, 8192), wanted.T, returned)
    cold_grad = pair_sum(local_cold)
    return (hot_grad, cold_grad, top_grad)


def solution(mesh):
    return jax.shard_map(
        body,
        mesh=mesh,
        in_specs=(
            P(("dp", "rep"), None),
            P(),
            P(),
            P(),
            P(),
            P("dp", None),
            P(("dp", "rep"), None),
            P(("dp", "rep"), None),
            P(("dp", "rep"), None),
            P(("dp", "rep")),
        ),
        out_specs=(P(), P("dp", None), P()),
        check_vma=False,
    )
```

profile of v0, /device:TPU:1, one launch (start us, length us, event | category | flops | bytes accessed | tf_op | source)
XLA Modules:
  0.0 227.3 jit_solution(2608019694409230883)
XLA Ops:
  2.3 3.4 %build_requests.1 = (s32[8,16,128]{2,1,0:T(8,128)S(1)}, s32[16,256]{1,0:T(8,128)S(1)}) custom-call(s32[256,13]{1,0:T(8,128)S(1)} %copy.23.owner_ref, s32[256,13]{1,0:T(8,128)S(1)} %copy.24.row_ref), custom_call_target="tpu_custom_call" | custom-call | tf_op jit(solution)/shard_map/build_requests/pallas_call | solution.py:242
  5.7 18.1 %exchange_requests.1 = s32[16,8,128]{2,1,0:T(8,128)S(1)} custom-call(s32[8,16,128]{2,1,0:T(8,128)S(1)} %get-tuple-element.14.query_ref), custom_call_target="tpu_custom_call" | custom-call | tf_op jit(solution)/shard_map/exchange_requests/pallas_call | solution.py:291
  23.8 1.2 copy-done.1
  25.0 10.7 %lookup_rows.1 = bf16[128,52,128]{2,1,0:T(8,128)(2,1)} custom-call(s32[128,128]{1,0:T(8,128)S(1)} %bitcast.9, bf16[4096,128]{1,0:T(8,128)(2,1)S(1)} %copy-done.1), custom_call_target="tpu_custom_call" | custom-call | tf_op jit(solution)/shard_map/lookup_rows/pallas_call | solution.py:331
  35.7 9.1 %all-to-all-start = ((bf16[128,52,128]{2,1,0:T(8,128)(2,1)}), bf16[128,52,128]{2,1,0:T(8,128)(2,1)}, u32[]{:S(2)}, u32[]{:S(2)}) async-start(bf16[128,52,128]{2,1,0:T(8,128)(2,1)} %lookup_rows.1), calls=%async_computation | async-start | bytes 3670016 | tf_op jit(solution)/shard_map/all_to_all | solution.py:608
  45.7 4.2 %gather_fusion = bf16[896,1024]{1,0:T(8,128)(2,1)} fusion(bf16[480,1024]{1,0:T(8,128)(2,1)S(1)} %concatenate.3, s32[1024]{0:T(1024)S(1)} %pad_clamp_fusion), kind=kCustom, calls=%fused_computation | custom fusion | bytes 3673600 | tf_op jit(solution)/shard_map/gather | solution.py:611
  50.0 5.5 %near_rows.1 = (bf16[32,112,128]{2,1,0:T(8,128)(2,1)S(1)}, bf16[256,128]{1,0:T(8,128)(2,1)S(1)}) custom-call(s32[13,256]{1,0:T(8,128)S(1)} %bitcast.14, bf16[4096,128]{1,0:T(8,128)(2,1)S(1)} %copy-done.2, bf16[256,256]{1,0:T(8,128)(2,1)S(1)} %copy-done.10, bf16[256,128]{1,0:T(8,128)(2,1)S(1)} %copy-done.12), custom_call_target="tpu_custom_call" | custom-call | tf_op jit(solution)/shard_map/near_rows/pallas_call | solution.py:363
  55.5 0.9 copy-done.3
  56.4 32.9 %all-to-all-done.got_ref = bf16[128,52,128]{2,1,0:T(8,128)(2,1)} async-done(((bf16[128,52,128]{2,1,0:T(8,128)(2,1)}), bf16[128,52,128]{2,1,0:T(8,128)(2,1)}, u32[]{:S(2)}, u32[]{:S(2)}) %all-to-all-start) | async-done | bytes 1703968 | tf_op jit(solution)/shard_map/all_to_all | solution.py:608
  89.3 1.2 copy-done.4
  90.5 33.4 %main_part.1 = (bf16[128,52,128]{2,1,0:T(8,128)(2,1)S(1)}, bf16[32,128,128]{2,1,0:T(8,128)(2,1)S(1)}, bf16[256,896]{1,0:T(8,128)(2,1)S(1)}, bf16[256,1024]{1,0:T(8,128)(2,1)S(1)}) custom-call(s32[16,256]{1,0:T(8,128)S(1)} %get-tuple-element.13.slot_ref, bf16[128,52,128]{2,1,0:T(8,128)(2,1)} %all-to-all-done.got_ref, bf16[32,112,128]{2,1,0:T(8,128)(2,1)S(1)} %copy-done.4, ...), custom_call_target="tpu_custom_call" | custom-call | tf_op jit(solution)/shard_map/main_part/pallas_call | solution.py:467
  123.9 1.2 copy-done
  125.9 6.4 %all-to-all-start.1 = ((bf16[128,52,128]{2,1,0:T(8,128)(2,1)}), bf16[128,52,128]{2,1,0:T(8,128)(2,1)S(1)}, u32[]{:S(2)}, u32[]{:S(2)}) async-start(bf16[128,52,128]{2,1,0:T(8,128)(2,1)} %copy-done), calls=%async_computation.1 | async-start | bytes 3670016 | tf_op jit(solution)/shard_map/all_to_all | solution.py:615
  133.1 1.0 pad.5
  134.8 0.9 copy.21
  135.7 1.7 copy.22
  138.1 1.1 reshape_reshape.3.index_ref
  139.9 1.0 copy-done.6
  141.7 7.7 %hot_and_top.1.in_ref = bf16[8192,128]{1,0:T(8,128)(2,1)S(1)} custom-call(s32[1,4096]{1,0:T(1,128)S(1)} %reshape_reshape.3.index_ref, s32[128,32]{1,0:T(8,128)S(1)} %bitcast.12, bf16[32,128,128]{2,1,0:T(8,128)(2,1)S(1)} %get-tuple-element.17.value_ref, bf16[256,128]{1,0:T(8,128)(2,1)S(1)} %get-tuple-element.16.bottom_ref, bf16[256,896]{1,0:T(8,128)(2,1)S(1)} %copy-done.6, ...), custom_call_target="tpu_custom_call" | custom-call | tf_op jit(solution)/shard_map/hot_and_top/pallas_call | solution.py:528
  149.5 59.1 %reduce_all.1.in_ref = bf16[8192,128]{1,0:T(8,128)(2,1)S(1)} custom-call(bf16[8192,128]{1,0:T(8,128)(2,1)S(1)} %hot_and_top.1.in_ref), custom_call_target="tpu_custom_call" | custom-call | tf_op jit(solution)/shard_map/reduce_all/pallas_call | solution.py:134
  208.6 2.2 format_sums.1
  210.8 12.2 %cold_sums.1.in_ref = f32[4096,128]{1,0:T(8,128)S(1)} custom-call(s32[1,8192]{1,0:T(1,128)S(1)} %copy-done.9, s32[128,128]{1,0:T(8,128)S(1)} %bitcast.13, bf16[128,52,128]{2,1,0:T(8,128)(2,1)S(1)} %all-to-all-done.1.value_ref), custom_call_target="tpu_custom_call" | custom-call | tf_op jit(solution)/shard_map/cold_sums/pallas_call | solution.py:559
  223.0 3.0 %pair_sum.1 = f32[4096,128]{1,0:T(8,128)S(1)} custom-call(f32[4096,128]{1,0:T(8,128)S(1)} %cold_sums.1.in_ref), custom_call_target="tpu_custom_call" | custom-call | tf_op jit(solution)/shard_map/pair_sum/pallas_call | solution.py:180
  226.0 1.3 copy.28
  (42 shorter events, 7.1 us)
Async XLA Ops:
  23.8 1.2 copy-start.1
  35.7 9.1 %copy-start.14 = (bf16[479,1024]{1,0:T(8,128)(2,1)S(1)}, bf16[479,1024]{1,0:T(8,128)(2,1)}, u32[]{:S(2)}) copy-start(bf16[479,1024]{1,0:T(8,128)(2,1)} %param.14) | copy-start | bytes 2942980
  35.7 53.6 %all-to-all-start = ((bf16[128,52,128]{2,1,0:T(8,128)(2,1)}), bf16[128,52,128]{2,1,0:T(8,128)(2,1)}, u32[]{:S(2)}, u32[]{:S(2)}) async-start(bf16[128,52,128]{2,1,0:T(8,128)(2,1)} %lookup_rows.1), calls=%async_computation | async-start | bytes 3670016 | tf_op jit(solution)/shard_map/all_to_all | solution.py:608
  44.8 0.7 copy-start.17
  44.8 0.8 copy-start.16
  44.8 0.8 copy-start.15
  45.7 4.2 %copy-start.2 = (bf16[4096,128]{1,0:T(8,128)(2,1)S(1)}, bf16[4096,128]{1,0:T(8,128)(2,1)}, u32[]{:S(2)}) copy-start(bf16[4096,128]{1,0:T(8,128)(2,1)} %table_ref.3) | copy-start | bytes 3145732
  45.7 4.2 %copy-start.10 = (bf16[256,256]{1,0:T(8,128)(2,1)S(1)}, bf16[256,256]{1,0:T(8,128)(2,1)}, u32[]{:S(2)}) copy-start(bf16[256,256]{1,0:T(8,128)(2,1)} %dense_ref.1) | copy-start | bytes 393220
  45.7 4.2 %copy-start.11 = (s32[256,13]{0,1:T(8,128)S(1)}, s32[256,13]{0,1:T(8,128)}, u32[]{:S(2)}) copy-start(s32[256,13]{0,1:T(8,128)} %param.18) | copy-start | bytes 39940
  45.7 4.2 %copy-start.12 = (bf16[256,128]{1,0:T(8,128)(2,1)S(1)}, bf16[256,128]{1,0:T(8,128)(2,1)}, u32[]{:S(2)}) copy-start(bf16[256,128]{1,0:T(8,128)(2,1)} %weight_ref.1) | copy-start | bytes 196612
  55.5 0.9 copy-start.3
  89.3 1.2 copy-start.4
  123.9 1.2 copy-start
  125.1 0.8 copy-start.5
  125.9 84.9 %all-to-all-start.1 = ((bf16[128,52,128]{2,1,0:T(8,128)(2,1)}), bf16[128,52,128]{2,1,0:T(8,128)(2,1)S(1)}, u32[]{:S(2)}, u32[]{:S(2)}) async-start(bf16[128,52,128]{2,1,0:T(8,128)(2,1)} %copy-done), calls=%async_computation.1 | async-start | bytes 3670016 | tf_op jit(solution)/shard_map/all_to_all | solution.py:615
  134.1 0.7 copy-start.13
  139.9 1.0 copy-start.6
  140.9 0.8 copy-start.7
  208.6 2.2 copy-start.8
  208.6 2.2 copy-start.9
where the time goes:
time: 228 us; the launch traced here: 227 us
  Pallas kernels  155 us (68%)
  waiting for transfers between devices  32.9 us (14%)
  local copies, waits for them, and re-layouts  22.7 us (10%)
  starting transfers between devices  15.5 us (7%)
    pallas_call x1, Pallas kernels, reduce_all(): pl.pallas_call(reduce_kernel, out_shape=jax.ShapeDtypeStruct((8192, 128),...  59.1 us
    pallas_call x1, Pallas kernels, main_part(): pl.pallas_call(main_kernel, out_shape=(jax.ShapeDtypeStruct((128, CAP, 12...  33.4 us
    all_to_all x1, waiting for transfers between devices, body(): lax.all_to_all(found_rows, 'dp', split_axis=0, concat_axis=0, tiled=True)  32.9 us
    pallas_call x1, Pallas kernels, exchange_requests(): pl.pallas_call(request_kernel, out_shape=jax.ShapeDtypeStruct((16, 8, 128...  18.1 us
    pallas_call x1, Pallas kernels, cold_sums(): pl.pallas_call(cold_kernel, out_shape=jax.ShapeDtypeStruct((4096, 128), F...  12.2 us
    unnamed x39, local copies, waits for them, and re-layouts  11.4 us
    pallas_call x1, Pallas kernels, lookup_rows(): pl.pallas_call(lookup_kernel, out_shape=jax.ShapeDtypeStruct((128, CAP, 1...  10.7 us
    all_to_all x1, starting transfers between devices, body(): lax.all_to_all(found_rows, 'dp', split_axis=0, concat_axis=0, tiled=True)  9.09 us
  transfers between devices with their start and end apart: 2, of which 1 were waited for; matrix products, arithmetic and copies ran while one was open for 5% of the time, Pallas kernels for 33%

commit v1 on v0

v1 whole, which is shorter than its diff:
```python
import jax
import jax.numpy as jnp
from jax import lax
from jax.experimental import pallas as pl
from jax.experimental.pallas import tpu as pltpu
from jax.sharding import PartitionSpec as P

MESH = pl.DeviceIdType.MESH
NX, NY, NZ = 4, 4, 8
VMEM_LIMIT = 48 * 1024 * 1024
F32 = jnp.float32
BF16 = jnp.bfloat16
CAP = 52
STRIDE = 56
EARLY = 48
UNROLL = 4


def place():
    me = lax.axis_index("dp")
    core = lax.axis_index("rep")
    z = lax.rem(me, NZ)
    x = lax.rem(lax.div(me, NZ), NX)
    y = lax.div(me, NZ * NX)
    return x, y, z, core


def peer(x, y, z, core):
    return (y * (NX * NZ) + x * NZ + z, core)


def rows_at(start, size):
    return pl.ds(pl.multiple_of(start, 16), size)


def reduce_kernel(in_ref, out_ref, core_buf, half, buf1, sum1, buf2, sum2, buf3, send_sem, recv_sem):
    x, y, z, core = place()
    partner = peer(x, y, z, 1 - core)
    xs = [peer(lax.rem(x + d, NX), y, z, core) for d in range(1, NX)]
    ys = [peer(x, lax.rem(y + d, NY), z, core) for d in range(1, NY)]
    zs = [peer(x, y, lax.rem(z + d, NZ), core) for d in range(1, NZ)]
    barrier = pltpu.get_barrier_semaphore()
    everyone = [partner] + xs + ys + zs
    for other in everyone:
        pl.semaphore_signal(barrier, inc=1, device_id=other, device_id_type=MESH)
    pl.semaphore_wait(barrier, len(everyone))

    started = []

    def send(src, dst, device):
        index = len(started)
        copy = pltpu.make_async_remote_copy(
            src_ref=src, dst_ref=dst, send_sem=send_sem.at[index], recv_sem=recv_sem.at[index],
            device_id=device, device_id_type=MESH,
        )
        copy.start()
        started.append(copy)
        return copy

    mine, other = core * 4096, (1 - core) * 4096
    own = (x, y)
    plan = [(which, d) for d in (1, 2, 3, 0) for which in (0, 1)]
    starts = [which * 2048 + lax.rem(own[which] + d, 4) * 512 for which, d in plan]
    over = [send(in_ref.at[rows_at(other + start, 512)], core_buf.at[rows_at(start, 512)], partner) for start in starts]
    first = {}
    for (which, d), start, copy in zip(plan, starts, over):
        copy.wait_recv()
        if d:

            @pl.loop(0, 2)
            def _(step):
                here = rows_at(start + step * 256, 256)
                value = in_ref[rows_at(mine + start + step * 256, 256), :].astype(F32)
                half[here, :] = (value + core_buf[here, :].astype(F32)).astype(BF16)

            first[which, d] = send(
                half.at[rows_at(start, 512)], buf1.at[which, d - 1], (xs, ys)[which][d - 1]
            )
    second = {}
    for which in range(2):
        for d in range(1, 4):
            first[which, d].wait_recv()
        for d in (1, 2, 3, 0):
            piece = lax.rem(own[1 - which] + d, 4) * 128
            here = rows_at(piece, 128)
            start = which * 2048 + own[which] * 512 + piece
            total = in_ref[rows_at(mine + start, 128), :].astype(F32) + core_buf[rows_at(start, 128), :].astype(F32)
            for e in range(3):
                total += buf1[which, e, here, :].astype(F32)
            if d:
                sum1[which, here, :] = total.astype(BF16)
                second[which, d] = send(sum1.at[which, here], buf2.at[which, d - 1], (ys, xs)[which][d - 1])
            else:
                sum2[:, which] = total.reshape(8, 16, 128)
    for which in range(2):
        for d in range(1, 4):
            second[which, d].wait_recv()
        sum2[:, which] = sum2[:, which] + (
            buf2[which, 0].astype(F32) + buf2[which, 1].astype(F32) + buf2[which, 2].astype(F32)
        ).reshape(8, 16, 128)
    third = [send(sum2.at[lax.rem(z + d, 8)], buf3.at[d - 1], zs[d - 1]) for d in range(1, 8)]
    for copy in third:
        copy.wait_recv()
    total = sum2[z]
    for d in range(7):
        total += buf3[d]
    base = (mine + x * 512 + y * 128, mine + 2048 + y * 512 + x * 128)
    back = {}
    for which in range(2):
        block = out_ref.at[rows_at(base[which] + z * 16, 16)]
        out_ref[rows_at(base[which] + z * 16, 16), :] = total[which].astype(BF16)
        for d in range(1, 8):
            back[which, d] = send(block, block, zs[d - 1])
    wide = {}
    for which in range(2):
        for d in range(1, 8):
            back[which, d].wait_recv()
        block = out_ref.at[rows_at(base[which], 128)]
        for d in range(1, 4):
            wide[which, d] = send(block, block, (ys, xs)[which][d - 1])
    last, across = {}, []
    for which in range(2):
        for d in range(1, 4):
            wide[which, d].wait_recv()
        block = out_ref.at[rows_at(mine + which * 2048 + own[which] * 512, 512)]
        for d in range(1, 4):
            last[which, d] = send(block, block, (xs, ys)[which][d - 1])
        across.append(send(block, block, partner))
    for d in range(1, 4):
        for which in range(2):
            last[which, d].wait_recv()
            block = out_ref.at[rows_at(mine + which * 2048 + lax.rem(own[which] + 4 - d, 4) * 512, 512)]
            across.append(send(block, block, partner))
    for copy in across:
        copy.wait_recv()
    for copy in started:
        copy.wait_send()


def reduce_all(values):
    return pl.pallas_call(
        reduce_kernel,
        out_shape=jax.ShapeDtypeStruct((8192, 128), BF16),
        in_specs=[pl.BlockSpec(memory_space=pltpu.VMEM)],
        out_specs=pl.BlockSpec(memory_space=pltpu.VMEM),
        scratch_shapes=[
            pltpu.VMEM((4096, 128), BF16),
            pltpu.VMEM((4096, 128), BF16),
            pltpu.VMEM((2, 3, 512, 128), BF16),
            pltpu.VMEM((2, 512, 128), BF16),
            pltpu.VMEM((2, 3, 128, 128), BF16),
            pltpu.VMEM((8, 2, 16, 128), F32),
            pltpu.VMEM((7, 2, 16, 128), F32),
            pltpu.SemaphoreType.DMA((61,)),
            pltpu.SemaphoreType.DMA((61,)),
        ],
        compiler_params=pltpu.CompilerParams(
            collective_id=0, has_side_effects=True, vmem_limit_bytes=VMEM_LIMIT
        ),
        name="reduce_all",
    )(values)


def pair_sum_kernel(in_ref, out_ref, got, send_sem, recv_sem):
    x, y, z, core = place()
    partner = peer(x, y, z, 1 - core)
    barrier = pltpu.get_barrier_semaphore()
    pl.semaphore_signal(barrier, inc=1, device_id=partner, device_id_type=MESH)
    pl.semaphore_wait(barrier, 1)
    copies = []
    for part in range(4):
        here = pl.ds(part * 1024, 1024)
        copy = pltpu.make_async_remote_copy(
            src_ref=in_ref.at[here], dst_ref=got.at[here], send_sem=send_sem.at[part],
            recv_sem=recv_sem.at[part], device_id=partner, device_id_type=MESH,
        )
        copy.start()
        copies.append(copy)
    for part in range(4):
        here = pl.ds(part * 1024, 1024)
        copies[part].wait()
        out_ref[here, :] = in_ref[here, :].astype(F32) + got[here, :].astype(F32)


def pair_sum(values):
    return pl.pallas_call(
        pair_sum_kernel,
        out_shape=jax.ShapeDtypeStruct((4096, 128), F32),
        in_specs=[pl.BlockSpec(memory_space=pltpu.VMEM)],
        out_specs=pl.BlockSpec(memory_space=pltpu.VMEM),
        scratch_shapes=[
            pltpu.VMEM((4096, 128), BF16),
            pltpu.SemaphoreType.DMA((4,)),
            pltpu.SemaphoreType.DMA((4,)),
        ],
        compiler_params=pltpu.CompilerParams(
            collective_id=1, has_side_effects=True, vmem_limit_bytes=VMEM_LIMIT
        ),
        name="pair_sum",
    )(values)


def params():
    return pltpu.CompilerParams(vmem_limit_bytes=VMEM_LIMIT)


def iota(shape, dimension):
    return lax.broadcasted_iota(jnp.int32, shape, dimension)


def build_kernel(owner_ref, row_ref, query_ref, slot_ref, place_ref, rank, rows, table):
    x, y, z, _ = place()
    fill = jnp.zeros((115, 256), F32)
    owner = jnp.concatenate([owner_ref[...].astype(F32), fill], axis=0).T.astype(jnp.int32)
    row = jnp.concatenate([row_ref[...].astype(F32), fill], axis=0).T
    dz = (lax.bitwise_and(owner, 7) - z + 8) & 7
    dx = (lax.bitwise_and(lax.shift_right_logical(owner, 3), 3) - x + 4) & 3
    dy = (lax.shift_right_logical(owner, 5) - y + 4) & 3
    relative = dz * 16 + dy * 4 + dx
    owner = owner.astype(F32)
    lane = iota((256, 128), 1)
    named = jnp.zeros((256, 128), F32)
    wanted = jnp.zeros((256, 128), F32)
    for f in range(13):
        here = relative[:, f : f + 1] == lane
        named = jnp.where(here, 1.0, named)
        wanted = jnp.where(here, row[:, f : f + 1], wanted)
    before = jnp.where(iota((256, 256), 1) < iota((256, 256), 0), 1.0, 0.0).astype(BF16)
    count = jnp.dot(before, named.astype(BF16), preferred_element_type=F32)
    back_x = (4 - dx) & 3
    block = ((((4 - dy) & 3) * 4 + back_x) * 8 + ((8 - dz) & 7)) * 64
    block, late = block.astype(F32), (4 * back_x).astype(F32)
    slots = jnp.zeros((256, 128), F32)
    places = jnp.zeros((256, 128), F32)
    for f in range(13):
        here = relative[:, f : f + 1] == lane
        mine = jnp.sum(jnp.where(here, count, 0.0), axis=1, keepdims=True)
        slots = jnp.where(lane == f, owner[:, f : f + 1] * STRIDE + mine, slots)
        inside = jnp.where(mine < float(EARLY), mine, mine + late[:, f : f + 1])
        places = jnp.where(lane == f, block[:, f : f + 1] + inside, places)
    slot_ref[...] = slots.T[0:16, :].astype(jnp.int32)
    place_ref[...] = places.T[0:16, :].astype(jnp.int32)
    rank[...] = jnp.where(named > 0.0, count, -1.0)
    rows[...] = wanted
    table[...] = jnp.zeros((128, 128), F32)

    for p in range(CAP):
        chosen = jnp.where(rank[...] == float(p), rows[...], 0.0)
        table[p : p + 1, :] = jnp.sum(chosen, axis=0, keepdims=True)

    query_ref[...] = table[...].T.astype(jnp.int32).reshape(8, 16, 128)


def build_requests(cold_owner, cold_row):
    return pl.pallas_call(
        build_kernel,
        out_shape=(
            jax.ShapeDtypeStruct((8, 16, 128), jnp.int32),
            jax.ShapeDtypeStruct((16, 256), jnp.int32),
            jax.ShapeDtypeStruct((16, 256), jnp.int32),
        ),
        scratch_shapes=[pltpu.VMEM((256, 128), F32), pltpu.VMEM((256, 128), F32), pltpu.VMEM((128, 128), F32)],
        compiler_params=params(),
        name="build_requests",
    )(cold_owner, cold_row)


def source_of(r, x, y, z):
    dz, dx, dy = lax.rem(r, 8), lax.rem(lax.div(r, 8), 4), lax.div(r, 32)
    return lax.rem(y - dy + 4, 4) * 32 + lax.rem(x - dx + 4, 4) * 8 + lax.rem(z - dz + 8, 8)


def widen(wide, ref, rows):
    @pl.loop(0, rows // 256)
    def _(step):
        here = pl.ds(pl.multiple_of(step * 256, 256), 256)
        wide[here, :] = ref[here, :].astype(F32)


def front_kernel(
    query_ref, table_ref, index_ref, hot_table_ref, dense_ref, weight_ref, top_ref,
    want_ref, got_ref, near_ref, bottom_ref, square_ref,
    tall, middle, turned, wanted, wide, wide_hot, held, chosen, passing, send_sem, recv_sem, local_sem,
):
    x, y, z, core = place()
    plane = [(dx, dy) for dy in range(4) for dx in range(4)]
    zs = [peer(x, y, lax.rem(z + d, NZ), core) for d in range(1, NZ)]
    xys = [peer(lax.rem(x + dx, NX), lax.rem(y + dy, NY), z, core) for dx, dy in plane[1:]]
    barrier = pltpu.get_barrier_semaphore()
    for other in zs + xys:
        pl.semaphore_signal(barrier, inc=1, device_id=other, device_id_type=MESH)
    widen(wide, table_ref, 4096)
    pl.semaphore_wait(barrier, len(zs) + len(xys))

    started = []

    def send(src, dst, device):
        index = len(started)
        copy = pltpu.make_async_remote_copy(
            src_ref=src, dst_ref=dst, send_sem=send_sem.at[index], recv_sem=recv_sem.at[index],
            device_id=device, device_id_type=MESH,
        )
        copy.start()
        started.append(copy)
        return copy

    copies = [send(query_ref.at[d], middle.at[d], zs[d - 1]) for d in range(1, 8)]
    middle[0] = query_ref[0]
    for copy in copies:
        copy.wait_recv()
    for d in range(8):
        for k in range(16):
            turned[k, d : d + 1, :] = middle[d, k : k + 1, :]
    copies = [send(turned.at[k], want_ref.at[k], xys[k - 1]) for k in range(1, 16)]
    want_ref[0] = turned[0]
    for copy in copies:
        copy.wait_recv()
    copy = pltpu.make_async_copy(want_ref, wanted, local_sem)
    copy.start()
    copy.wait()

    order = (2, 1, 3, 0)
    along = {}
    copies = []

    def collect(dy):
        @pl.loop(0, 8)
        def _(d):
            back = lax.rem(8 - d, 8)
            for tile in range(13):
                rows = []
                for e in range(16):
                    dx, p = (tile // 3, tile % 3 * 16 + e) if tile < 12 else (e // 4, EARLY + e % 4)
                    k = (4 - dy) % 4 * 4 + (4 - dx) % 4
                    rows.append(wide[pl.ds(wanted[k, back, p], 1), :])
                chosen[dy, d, tile * 16 : tile * 16 + 16, :] = jnp.concatenate(rows, axis=0).astype(BF16)

        for d in range(1, 8):
            along[dy, d] = send(chosen.at[dy, d], passing.at[dy, d], zs[d - 1])
        passing[dy, 0] = chosen[dy, 0]

    def pass_on(dy):
        for d in range(1, 8):
            along[dy, d].wait_recv()
        for dx in range(4):
            early = passing.at[dy, :, pl.ds(dx * EARLY, EARLY)]
            late = passing.at[dy, :, pl.ds(4 * EARLY, 16)]
            k = dy * 4 + dx
            if k:
                copies.append(send(early, got_ref.at[k, :, pl.ds(0, EARLY)], xys[k - 1]))
                copies.append(send(late, got_ref.at[k, :, pl.ds(EARLY, 16)], xys[k - 1]))
            else:
                got_ref[0, :, 0:EARLY, :] = passing[0, :, 0:EARLY, :]
                got_ref[0, :, EARLY:64, :] = passing[0, :, 4 * EARLY : 4 * EARLY + 16, :]

    collect(order[0])
    collect(order[1])
    widen(wide_hot, hot_table_ref, 4096)
    bottom = jnp.maximum(jnp.dot(dense_ref[...], weight_ref[...], preferred_element_type=F32), 0.0)
    bottom_ref[...] = bottom.astype(BF16)
    held[...] = bottom

    @pl.loop(0, 32)
    def _(g):
        near_ref[g, 0:16, :] = jnp.concatenate(
            [held[pl.ds(pl.multiple_of(g * 8, 8), 8), :]]
            + [wide_hot[pl.ds(index_ref[0, g * 8 + k], 1), :] for k in range(8)], axis=0
        ).astype(BF16)
        for f in range(1, 13, 2):
            rows = [wide_hot[pl.ds(index_ref[f + k // 8, g * 8 + k % 8], 1), :] for k in range(16)]
            near_ref[g, 8 + f * 8 : 24 + f * 8, :] = jnp.concatenate(rows, axis=0).astype(BF16)

    pass_on(order[0])
    collect(order[2])
    pass_on(order[1])
    collect(order[3])
    tall[464:512, :] = jnp.zeros((48, 1024), BF16)
    tall[0:479, :] = top_ref[...]

    @pl.loop(0, 7)
    def _(b):
        i = 4 * b + (iota((128, 512), 0) >> 5)
        j = iota((128, 512), 0) & 31
        high, low = jnp.maximum(i, j), jnp.minimum(i, j)
        source = 128 + ((high * (high - 1)) >> 1) + low
        source = jnp.where((high == low) | (high > 26), -1, source)
        pick = jnp.where(source == iota((128, 512), 1), 1.0, 0.0).astype(BF16)
        square_ref[pl.ds(pl.multiple_of(b * 128, 128), 128), :] = jnp.dot(
            pick, tall[...], preferred_element_type=F32
        ).astype(BF16)

    pass_on(order[2])
    pass_on(order[3])
    for copy in copies:
        copy.wait_recv()
    for copy in started:
        copy.wait_send()


def front_part(query, table, hot_index, hot_table, dense, weight, top):
    vmem = pl.BlockSpec(memory_space=pltpu.VMEM)
    return pl.pallas_call(
        front_kernel,
        out_shape=(
            jax.ShapeDtypeStruct((16, 8, 128), jnp.int32),
            jax.ShapeDtypeStruct((16, 8, 64, 128), BF16),
            jax.ShapeDtypeStruct((32, 112, 128), BF16),
            jax.ShapeDtypeStruct((256, 128), BF16),
            jax.ShapeDtypeStruct((896, 1024), BF16),
        ),
        in_specs=[vmem, vmem, pl.BlockSpec(memory_space=pltpu.SMEM), vmem, vmem, vmem, vmem],
        out_specs=(vmem,) * 5,
        scratch_shapes=[
            pltpu.VMEM((512, 1024), BF16),
            pltpu.VMEM((8, 16, 128), jnp.int32),
            pltpu.VMEM((16, 8, 128), jnp.int32),
            pltpu.SMEM((16, 8, 128), jnp.int32),
            pltpu.VMEM((4096, 128), F32),
            pltpu.VMEM((4096, 128), F32),
            pltpu.VMEM((256, 128), F32),
            pltpu.VMEM((4, 8, 208, 128), BF16),
            pltpu.VMEM((4, 8, 208, 128), BF16),
            pltpu.SemaphoreType.DMA((80,)),
            pltpu.SemaphoreType.DMA((80,)),
            pltpu.SemaphoreType.DMA,
        ],
        compiler_params=pltpu.CompilerParams(collective_id=2, has_side_effects=True, vmem_limit_bytes=VMEM_LIMIT),
        name="front_part",
    )(query, table, hot_index, hot_table, dense, weight, top)


def main_kernel(
    slot_ref, place_ref, got_ref, near_ref, bottom_ref, weight0_ref, weight_ref, out_weight_ref, click_ref,
    sent_ref, hot_ref, low_ref, grad_ref,
    wide, stack, far, pairs, hidden, slope, terms,
):
    widen(wide, got_ref, 8192)
    for e in range(UNROLL):
        far[e, 104:144, :] = jnp.zeros((40, 128), F32)
    same = (iota((256, 256), 0) & 7) == (iota((256, 256), 1) & 7)
    fold = jnp.where((iota((256, 128), 0) >> 3) == (iota((256, 128), 1) & 31), 1.0, 0.0).astype(BF16)
    unfold = jnp.where((iota((128, 256), 1) >> 3) == (iota((128, 256), 0) & 31), 1.0, 0.0).astype(BF16)
    quarter = iota((8, 128), 1) >> 5
    zero8 = jnp.zeros((8, 128), F32)

    @pl.loop(0, 32 // UNROLL)
    def _(step):
        groups = [step * UNROLL + e for e in range(UNROLL)]
        for e, g in enumerate(groups):
            for f in range(13):
                for k in range(8):
                    far[e, f * 8 + k : f * 8 + k + 1, :] = wide[pl.ds(place_ref[f, g * 8 + k], 1), :]
        values = [jnp.concatenate([near_ref[g], far[e].astype(BF16)], axis=0) for e, g in enumerate(groups)]
        dots = [
            lax.dot_general(value, value, (((1,), (1,)), ((), ())), preferred_element_type=F32) for value in values
        ]
        dots = [jnp.where(same, dot, 0.0).astype(BF16) for dot in dots]
        folds = [jnp.dot(dot, fold, preferred_element_type=F32) for dot in dots]
        for e, g in enumerate(groups):
            stack[g] = values[e]
            for b in range(7):
                block = zero8
                for q in range(4):
                    i = 4 * b + q
                    block = jnp.where(quarter == q, folds[e][i * 8 : i * 8 + 8, :], block)
                pairs[pl.ds(pl.multiple_of(g * 8, 8), 8), b * 128 : b * 128 + 128] = block

    for b in range(7):
        i = 4 * b + (iota((256, 128), 1) >> 5)
        j = iota((256, 128), 1) & 31
        low_ref[:, b * 128 : b * 128 + 128] = jnp.where(i > j, pairs[:, b * 128 : b * 128 + 128], 0.0).astype(BF16)

    total = jnp.zeros((256, 128), F32)
    for n in range(4):
        here = slice(n * 256, n * 256 + 256)
        hidden[:, here] = jnp.dot(bottom_ref[...], weight0_ref[0:128, here], preferred_element_type=F32) + jnp.dot(
            low_ref[...], weight_ref[:, here], preferred_element_type=F32
        )
    for n in range(8):
        here = slice(n * 128, n * 128 + 128)
        v = hidden[:, here]
        c = 0.7978845608028654
        square = v * v
        t = jnp.tanh(c * v * (1.0 + 0.044715 * square))
        weight = out_weight_ref[:, here].astype(F32)
        act = (0.5 * v * (1.0 + t)).astype(BF16).astype(F32)
        total = total + act * weight
        slope[:, here] = weight * (0.5 * (1.0 + t) + 0.5 * c * v * (1.0 - t * t) * (1.0 + 0.134145 * square))
    logits = jnp.sum(total, axis=1, keepdims=True)
    clicks = jnp.broadcast_to(click_ref[...].astype(F32), (128, 256)).T[:, 0:1]
    errors = 1.0 / (1.0 + jnp.exp(-logits)) - clicks
    grad_ref[...] = (slope[...] * errors).astype(BF16)
    for b in range(7):
        here = slice(b * 128, b * 128 + 128)
        pairs[:, here] = lax.dot_general(
            grad_ref[...], weight_ref[here, :], (((1,), (1,)), ((), ())), preferred_element_type=F32
        )

    @pl.loop(0, 7)
    def _(step):
        wide[pl.ds(pl.multiple_of(step * 1024, 1024), 1024), :] = jnp.zeros((1024, 128), F32)

    @pl.loop(0, 32 // UNROLL)
    def _(step):
        groups = [step * UNROLL + e for e in range(UNROLL)]
        spreads = []
        for g in groups:
            rows = []
            for b in range(7):
                block = pairs[pl.ds(pl.multiple_of(g * 8, 8), 8), b * 128 : b * 128 + 128]
                for q in range(4):
                    rows.append(jnp.where(quarter == q, block, 0.0))
            rows += [zero8] * 4
            spreads.append(jnp.concatenate(rows, axis=0).astype(BF16))
        spreads = [jnp.dot(spread, unfold, preferred_element_type=F32) for spread in spreads]
        spreads = [jnp.where(same, spread, 0.0).astype(BF16) for spread in spreads]
        results = [jnp.dot(spread, stack[g], preferred_element_type=F32) for spread, g in zip(spreads, groups)]
        for e, g in enumerate(groups):
            for f in range(13):
                hot_ref[f, pl.ds(pl.multiple_of(g * 8, 8), 8), :] = results[e][8 + f * 8 : 16 + f * 8, :]
            terms[e] = results[e][112:216, :]
        for e, g in enumerate(groups):
            for f in range(13):
                for k in range(8):
                    row = f * 8 + k
                    wide[pl.ds(slot_ref[f, g * 8 + k], 1), :] = terms[e, row : row + 1, :]

    @pl.loop(0, 16)
    def _(step):
        for e in range(8):
            d = step * 8 + e
            sent_ref[d] = wide[pl.ds(pl.multiple_of(d * STRIDE, 8), CAP), :].astype(BF16)


def main_part(slot, places, got, near, bottom, weight0, weight, out_weight, clicks):
    vmem = pl.BlockSpec(memory_space=pltpu.VMEM)
    return pl.pallas_call(
        main_kernel,
        out_shape=(
            jax.ShapeDtypeStruct((128, CAP, 128), BF16),
            jax.ShapeDtypeStruct((13, 256, 128), F32),
            jax.ShapeDtypeStruct((256, 896), BF16),
            jax.ShapeDtypeStruct((256, 1024), BF16),
        ),
        in_specs=[pl.BlockSpec(memory_space=pltpu.SMEM)] * 2 + [vmem] * 7,
        out_specs=(vmem,) * 4,
        scratch_shapes=[
            pltpu.VMEM((8192, 128), F32),
            pltpu.VMEM((32, 256, 128), BF16),
            pltpu.VMEM((UNROLL, 144, 128), F32),
            pltpu.VMEM((256, 896), F32),
            pltpu.VMEM((256, 1024), F32),
            pltpu.VMEM((256, 1024), F32),
            pltpu.VMEM((UNROLL, 104, 128), F32),
        ],
        compiler_params=params(),
        name="main_part",
    )(slot, places, got, near, bottom, weight0, weight, out_weight, clicks)


def hot_kernel(row_ref, value_ref, bottom_ref, low_ref, grad_ref, out_ref, halves, top):
    columns = jnp.concatenate([(row_ref[...] >> 11).astype(F32), jnp.zeros((115, 256), F32)], axis=0).T
    for f in range(13):
        high = columns[:, f : f + 1]
        value = value_ref[f]
        halves[f * 256 : f * 256 + 256, 0:128] = jnp.where(high == 0.0, value, 0.0).astype(BF16)
        halves[f * 256 : f * 256 + 256, 128:256] = jnp.where(high == 0.0, 0.0, value).astype(BF16)

    @pl.loop(0, 8)
    def _(m):
        start = pl.multiple_of(m * 256, 256)
        wanted = iota((256, 256), 0) + m * 256
        hits = [
            jnp.where((jnp.broadcast_to(row_ref[f : f + 1, :], (256, 256)) & 2047) == wanted, 1.0, 0.0).astype(BF16)
            for f in range(13)
        ]
        total = jnp.dot(jnp.concatenate(hits, axis=1), halves[...], preferred_element_type=F32)
        out_ref[pl.ds(start, 256), :] = total[:, 0:128].astype(BF16)
        out_ref[pl.ds(start + 2048, 256), :] = total[:, 128:256].astype(BF16)

    top[472:480, :] = jnp.zeros((8, 1024), F32)
    top[0:128, :] = lax.dot_general(
        bottom_ref[...], grad_ref[...], (((0,), (0,)), ((), ())), preferred_element_type=F32
    )
    for b in range(7):
        part = lax.dot_general(
            low_ref[:, b * 128 : b * 128 + 128], grad_ref[...], (((0,), (0,)), ((), ())), preferred_element_type=F32
        )
        for q in range(4):
            i = 4 * b + q
            if 0 < i < 27:
                at = 128 + i * (i - 1) // 2
                top[at : at + i, :] = part[q * 32 : q * 32 + i, :]
    for n in range(8):
        out_ref[4096 + n * 480 : 4576 + n * 480, :] = top[:, n * 128 : n * 128 + 128].astype(BF16)
    out_ref[7936:8192, :] = jnp.zeros((256, 128), BF16)


def hot_and_top(row, value, bottom, low, grad):
    return pl.pallas_call(
        hot_kernel,
        out_shape=jax.ShapeDtypeStruct((8192, 128), BF16),
        scratch_shapes=[pltpu.VMEM((3328, 256), BF16), pltpu.VMEM((480, 1024), F32)],
        compiler_params=params(),
        name="hot_and_top",
    )(row, value, bottom, low, grad)


def cold_kernel(want_ref, value_ref, out_ref, halves, joined):
    x, y, z, _ = place()
    pad = jnp.zeros((64 - CAP, 128), F32)
    even, odd = want_ref[pl.ds(0, 64, stride=2), :], want_ref[pl.ds(1, 64, stride=2), :]
    joined[...] = jnp.where(iota((64, 128), 1) < 64, even, pltpu.roll(odd, 64, 1)) & 2047
    columns = (want_ref[...] >> 11).astype(F32).T
    for r in range(128):
        high = columns[0:64, r : r + 1]
        value = jnp.concatenate([value_ref[source_of(r, x, y, z)].astype(F32), pad], axis=0)
        halves[r * 64 : r * 64 + 64, 0:128] = jnp.where(high == 0.0, value, 0.0).astype(BF16)
        halves[r * 64 : r * 64 + 64, 128:256] = jnp.where(high == 0.0, 0.0, value).astype(BF16)

    @pl.loop(0, 8)
    def _(m):
        start = pl.multiple_of(m * 256, 256)
        wanted = iota((256, 128), 0) + m * 256
        total = jnp.zeros((256, 256), F32)
        for n in range(4):
            hits = [
                jnp.where(jnp.broadcast_to(joined[t : t + 1, :], (256, 128)) == wanted, 1.0, 0.0).astype(BF16)
                for t in range(n * 16, n * 16 + 16)
            ]
            total = total + jnp.dot(
                jnp.concatenate(hits, axis=1), halves[n * 2048 : n * 2048 + 2048, :], preferred_element_type=F32
            )
        out_ref[pl.ds(start, 256), :] = total[:, 0:128].astype(BF16)
        out_ref[pl.ds(start + 2048, 256), :] = total[:, 128:256].astype(BF16)


def cold_sums(want, value):
    return pl.pallas_call(
        cold_kernel,
        out_shape=jax.ShapeDtypeStruct((4096, 128), BF16),
        scratch_shapes=[pltpu.VMEM((8192, 256), BF16), pltpu.VMEM((64, 128), jnp.int32)],
        compiler_params=params(),
        name="cold_sums",
    )(want, value)


def format_kernel(in_ref, hot_ref, top_ref):
    hot_ref[...] = in_ref[0:4096, :].astype(F32)
    for n in range(8):
        top_ref[:, n * 128 : n * 128 + 128] = in_ref[4096 + n * 480 : 4576 + n * 480, :].astype(F32)[0:479, :]


def format_sums(values):
    return pl.pallas_call(
        format_kernel,
        out_shape=(jax.ShapeDtypeStruct((4096, 128), F32), jax.ShapeDtypeStruct((479, 1024), F32)),
        compiler_params=params(),
        name="format_sums",
    )(values)


def body(
    dense_feats,
    bottom_weight,
    top_weight,
    out_weight,
    hot_table,
    cold_table,
    hot_index,
    cold_owner,
    cold_row,
    clicks,
):
    query, slot, places = build_requests(cold_owner.T, cold_row.T)
    hot_fields = hot_index.T
    wanted, got, near, bottom, weight = front_part(
        query, cold_table, hot_fields, hot_table, dense_feats, bottom_weight, top_weight
    )
    wanted = wanted.reshape(128, 128)
    outgoing, hot_terms, low, grad = main_part(
        slot, places, got.reshape(8192, 128), near, bottom, top_weight, weight, out_weight.reshape(1, 1024), clicks.reshape(1, 256)
    )
    returned = lax.all_to_all(outgoing, "dp", split_axis=0, concat_axis=0, tiled=True)
    sums = hot_and_top(hot_fields, hot_terms, bottom, low, grad)
    hot_grad, top_grad = format_sums(reduce_all(sums))
    local_cold = cold_sums(wanted, returned)
    cold_grad = pair_sum(local_cold)
    return (hot_grad, cold_grad, top_grad)


def solution(mesh):
    return jax.shard_map(
        body,
        mesh=mesh,
        in_specs=(
            P(("dp", "rep"), None),
            P(),
            P(),
            P(),
            P(),
            P("dp", None),
            P(("dp", "rep"), None),
            P(("dp", "rep"), None),
            P(("dp", "rep"), None),
            P(("dp", "rep")),
        ),
        out_specs=(P(), P("dp", None), P()),
        check_vma=False,
    )
```

time: 228 us -> 200 us (0.88)
  waiting for transfers between devices: 32.9 us -> 0.01 us
  Pallas kernels: 155 us -> 174 us
  local copies, waits for them, and re-layouts: 22.7 us -> 14 us
  starting transfers between devices: 15.5 us -> 10.9 us
    pallas_call x4 -> x2, Pallas kernels: 46.5 us -> 80 us  [the longest x1 68.5 us: front_part(): pl.pallas_call(front_kernel, out_shape=(jax.ShapeDtypeStruct((16, 8, 128)...]
    all_to_all x1 -> x0, waiting for transfers between devices: 32.9 us -> none  [body(): lax.all_to_all(found_rows, 'dp', split_axis=0, concat_axis=0, tiled=True)]
    pallas_call x1, Pallas kernels: 33.4 us -> 21.5 us  [main_part(): pl.pallas_call(main_kernel, out_shape=(jax.ShapeDtypeStruct((128, CAP, 12...]
    all_to_all x1 -> x0, starting transfers between devices: 9.09 us -> none  [body(): lax.all_to_all(found_rows, 'dp', split_axis=0, concat_axis=0, tiled=True)]
    all_to_all x1, starting transfers between devices: 6.42 us -> 10.9 us  [body(): lax.all_to_all(outgoing, 'dp', split_axis=0, concat_axis=0, tiled=True)]
    gather x1 -> x0, local copies, waits for them, and re-layouts: 4.19 us -> none  [body(): jnp.concatenate([top_weight, jnp.zeros((1, 1024), BF16)], axis=0)]
    pad x3 -> x0, local copies, waits for them, and re-layouts: 3.51 us -> none  [body(): jnp.pad(hot_fields.reshape(13, 32, 8).transpose(1, 0, 2), ((0, 0), (1, 2)...]
    reshape x4 -> x0, local copies, waits for them, and re-layouts: 2.38 us -> none  [the longest x1 0.84 us: body(): hot_fields.reshape(13, 32, 8).transpose(1, 0, 2)]
  transfers between devices with their start and end apart: 2 -> 1, of which waited for: 1 -> 0; matrix products, arithmetic and copies ran while one was open for 5% -> 0% of each run, Pallas kernels for 33% -> 33%
where the time goes in v1:
time: 200 us
  Pallas kernels  174 us (87%)
  local copies, waits for them, and re-layouts  14 us (7%)
  starting transfers between devices  10.9 us (5%)
    pallas_call x1, Pallas kernels, front_part(): pl.pallas_call(front_kernel, out_shape=(jax.ShapeDtypeStruct((16, 8, 128)...  68.5 us
    pallas_call x1, Pallas kernels, reduce_all(): pl.pallas_call(reduce_kernel, out_shape=jax.ShapeDtypeStruct((8192, 128),...  57 us
    pallas_call x1, Pallas kernels, main_part(): pl.pallas_call(main_kernel, out_shape=(jax.ShapeDtypeStruct((128, CAP, 12...  21.5 us
    unnamed x39, local copies, waits for them, and re-layouts  13.3 us
    pallas_call x1, Pallas kernels, cold_sums(): pl.pallas_call(cold_kernel, out_shape=jax.ShapeDtypeStruct((4096, 128), B...  11.4 us
    all_to_all x1, starting transfers between devices, body(): lax.all_to_all(outgoing, 'dp', split_axis=0, concat_axis=0, tiled=True)  10.9 us
    pallas_call x1, Pallas kernels, hot_and_top(): pl.pallas_call(hot_kernel, out_shape=jax.ShapeDtypeStruct((8192, 128), BF...  6.35 us
    pallas_call x1, Pallas kernels, build_requests(): pl.pallas_call(build_kernel, out_shape=(jax.ShapeDtypeStruct((8, 16, 128)...  4.09 us
  transfers between devices with their start and end apart: 1, of which 0 were waited for; matrix products, arithmetic and copies ran while one was open for 0% of the time, Pallas kernels for 33%

profile of v1, /device:TPU:1, one launch (start us, length us, event | category | flops | bytes accessed | tf_op | source)
XLA Modules:
  0.0 199.7 jit_solution(2228555673525173696)
XLA Ops:
  0.6 0.7 reshape.19.out_weight_ref
  1.3 0.7 copy-done.16
  2.1 0.7 copy-done.17
  2.8 4.1 %build_requests.1 = (s32[8,16,128]{2,1,0:T(8,128)S(1)}, s32[16,256]{1,0:T(8,128)S(1)}, s32[16,256]{1,0:T(8,128)S(1)}) custom-call(s32[13,256]{1,0:T(8,128)S(1)} %bitcast.9, s32[13,256]{1,0:T(8,128)S(1)} %bitcast.10), custom_call_target="tpu_custom_call" | custom-call | tf_op jit(solution)/shard_map/build_requests/pallas_call | solution.py:255
  6.9 1.2 copy-done
  8.1 1.2 copy-done.2
  9.3 1.2 copy-done.3
  10.5 0.9 copy-done.10
  11.4 0.7 copy-done.11
  12.1 0.8 copy-done.13
  13.0 68.5 %front_part.1 = (s32[16,8,128]{2,1,0:T(8,128)S(1)}, bf16[16,8,64,128]{3,2,1,0:T(8,128)(2,1)}, bf16[32,112,128]{2,1,0:T(8,128)(2,1)S(1)}, bf16[256,128]{1,0:T(8,128)(2,1)S(1)}, bf16[896,1024]{1,0:T(8,128)(2,1)}) custom-call(s32[8,16,128]{2,1,0:T(8,128)S(1)} %get-tuple-element.19.query_ref, bf16[4096,128]{1,0:T(8,128)(2,1)S(1)} %copy-done.2, ...), custom_call_target="tpu_custom_call" | custom-call | tf_op jit(solution)/shard_map/front_part/pallas_call | solution.py:402
  81.6 21.5 %main_part.1 = (bf16[128,52,128]{2,1,0:T(8,128)(2,1)}, f32[13,256,128]{2,1,0:T(8,128)S(1)}, bf16[256,896]{1,0:T(8,128)(2,1)S(1)}, bf16[256,1024]{1,0:T(8,128)(2,1)S(1)}) custom-call(s32[16,256]{1,0:T(8,128)S(1)} %get-tuple-element.17.slot_ref, s32[16,256]{1,0:T(8,128)S(1)} %get-tuple-element.18.place_ref, bf16[8192,128]{1,0:T(8,128)(2,1)} %bitcast.12, ...), custom_call_target="tpu_custom_call" | custom-call | tf_op jit(solution)/shard_map/main_part/pallas_call | solution.py:537
  103.1 0.8 copy-done.4
  103.9 0.8 copy-done.6
  104.7 10.9 %all-to-all-start = ((bf16[128,52,128]{2,1,0:T(8,128)(2,1)}), bf16[128,52,128]{2,1,0:T(8,128)(2,1)S(1)}, u32[]{:S(2)}, u32[]{:S(2)}) async-start(bf16[128,52,128]{2,1,0:T(8,128)(2,1)} %get-tuple-element.29), calls=%async_computation | async-start | bytes 3670016 | tf_op jit(solution)/shard_map/all_to_all | solution.py:684
  115.6 1.0 copy-done.5
  116.7 1.0 copy-done.7
  117.7 0.8 copy-done.9
  118.5 6.4 %hot_and_top.1.in_ref = bf16[8192,128]{1,0:T(8,128)(2,1)S(1)} custom-call(s32[13,256]{1,0:T(8,128)S(1)} %bitcast.7, f32[13,256,128]{2,1,0:T(8,128)S(1)} %get-tuple-element.24.value_ref, bf16[256,128]{1,0:T(8,128)(2,1)S(1)} %copy-done.9, bf16[256,896]{1,0:T(8,128)(2,1)S(1)} %copy-done.7, bf16[256,1024]{1,0:T(8,128)(2,1)S(1)} %copy-done.5), custom_call_target="tpu_custom_call" | custom-call | tf_op jit(solution)/shard_map/hot_and_top/pallas_call | solution.py:600
  124.9 57.0 %reduce_all.1.in_ref = bf16[8192,128]{1,0:T(8,128)(2,1)S(1)} custom-call(bf16[8192,128]{1,0:T(8,128)(2,1)S(1)} %hot_and_top.1.in_ref), custom_call_target="tpu_custom_call" | custom-call | tf_op jit(solution)/shard_map/reduce_all/pallas_call | solution.py:141
  181.9 2.2 %format_sums.1 = (f32[4096,128]{1,0:T(8,128)}, f32[479,1024]{1,0:T(8,128)}) custom-call(bf16[8192,128]{1,0:T(8,128)(2,1)S(1)} %reduce_all.1.in_ref), custom_call_target="tpu_custom_call" | custom-call | tf_op jit(solution)/shard_map/format_sums/pallas_call | solution.py:655
  184.0 11.4 %cold_sums.1.in_ref = bf16[4096,128]{1,0:T(8,128)(2,1)S(1)} custom-call(s32[128,128]{1,0:T(8,128)S(1)} %bitcast.8, bf16[128,52,128]{2,1,0:T(8,128)(2,1)S(1)} %all-to-all-done.value_ref), custom_call_target="tpu_custom_call" | custom-call | tf_op jit(solution)/shard_map/cold_sums/pallas_call | solution.py:639
  195.5 2.9 %pair_sum.1 = f32[4096,128]{1,0:T(8,128)S(1)} custom-call(bf16[4096,128]{1,0:T(8,128)(2,1)S(1)} %cold_sums.1.in_ref), custom_call_target="tpu_custom_call" | custom-call | tf_op jit(solution)/shard_map/pair_sum/pallas_call | solution.py:186
  198.4 1.3 copy.14
  (26 shorter events, 0.1 us)
Async XLA Ops:
  0.6 80.9 %copy-start.18 = (s32[256]{0:T(256)S(1)}, s32[256]{0:T(256)}, u32[]{:S(2)}) copy-start(s32[256]{0:T(256)} %param.19) | copy-start | bytes 3076
  1.3 0.7 copy-start.16
  2.1 0.7 copy-start.17
  6.9 1.2 copy-start
  8.1 1.2 copy-start.2
  9.3 1.2 copy-start.3
  10.5 0.9 copy-start.10
  11.4 0.7 copy-start.11
  12.1 0.8 copy-start.13
  13.0 68.6 %copy-start.1 = (bf16[479,1024]{1,0:T(8,128)(2,1)S(1)}, bf16[479,1024]{1,0:T(8,128)(2,1)}, u32[]{:S(2)}) copy-start(bf16[479,1024]{1,0:T(8,128)(2,1)} %weight0_ref.1) | copy-start | bytes 2942980
  81.5 21.6 %copy-start.8 = (bf16[256,128]{1,0:T(8,128)(2,1)}, bf16[256,128]{1,0:T(8,128)(2,1)S(1)}, u32[]{:S(2)}) copy-start(bf16[256,128]{1,0:T(8,128)(2,1)S(1)} %get-tuple-element.22.bottom_ref) | copy-start | bytes 196612
  81.5 21.6 %copy-start.14 = (s32[16,8,128]{2,1,0:T(8,128)}, s32[16,8,128]{2,1,0:T(8,128)S(1)}, u32[]{:S(2)}) copy-start(s32[16,8,128]{2,1,0:T(8,128)S(1)} %get-tuple-element.28) | copy-start | bytes 196612
  103.1 0.8 copy-start.4
  103.9 0.8 copy-start.6
  104.7 10.9 %copy-start.12 = (s32[256,13]{0,1:T(8,128)S(1)}, s32[256,13]{0,1:T(8,128)}, u32[]{:S(2)}) copy-start(s32[256,13]{0,1:T(8,128)} %param.16) | copy-start | bytes 39940
  104.7 79.4 %all-to-all-start = ((bf16[128,52,128]{2,1,0:T(8,128)(2,1)}), bf16[128,52,128]{2,1,0:T(8,128)(2,1)S(1)}, u32[]{:S(2)}, u32[]{:S(2)}) async-start(bf16[128,52,128]{2,1,0:T(8,128)(2,1)} %get-tuple-element.29), calls=%async_computation | async-start | bytes 3670016 | tf_op jit(solution)/shard_map/all_to_all | solution.py:684
  115.6 1.0 copy-start.5
  116.7 1.0 copy-start.7
  117.7 0.8 copy-start.9
  181.8 2.2 %copy-start.15 = (s32[16,8,128]{2,1,0:T(8,128)S(1)}, s32[16,8,128]{2,1,0:T(8,128)}, u32[]{:S(2)}) copy-start(s32[16,8,128]{2,1,0:T(8,128)} %copy-done.14) | copy-start | bytes 196612

commit v2 on v1

--- a/solution.py
+++ b/solution.py
@@ -11,7 +11,6 @@
 F32 = jnp.float32
 BF16 = jnp.bfloat16
 CAP = 52
-STRIDE = 56
 EARLY = 48
 UNROLL = 4
 
@@ -31,173 +30,6 @@
 
 def rows_at(start, size):
     return pl.ds(pl.multiple_of(start, 16), size)
-
-
-def reduce_kernel(in_ref, out_ref, core_buf, half, buf1, sum1, buf2, sum2, buf3, send_sem, recv_sem):
-    x, y, z, core = place()
-    partner = peer(x, y, z, 1 - core)
-    xs = [peer(lax.rem(x + d, NX), y, z, core) for d in range(1, NX)]
-    ys = [peer(x, lax.rem(y + d, NY), z, core) for d in range(1, NY)]
-    zs = [peer(x, y, lax.rem(z + d, NZ), core) for d in range(1, NZ)]
-    barrier = pltpu.get_barrier_semaphore()
-    everyone = [partner] + xs + ys + zs
-    for other in everyone:
-        pl.semaphore_signal(barrier, inc=1, device_id=other, device_id_type=MESH)
-    pl.semaphore_wait(barrier, len(everyone))
-
-    started = []
-
-    def send(src, dst, device):
-        index = len(started)
-        copy = pltpu.make_async_remote_copy(
-            src_ref=src, dst_ref=dst, send_sem=send_sem.at[index], recv_sem=recv_sem.at[index],
-            device_id=device, device_id_type=MESH,
-        )
-        copy.start()
-        started.append(copy)
-        return copy
-
-    mine, other = core * 4096, (1 - core) * 4096
-    own = (x, y)
-    plan = [(which, d) for d in (1, 2, 3, 0) for which in (0, 1)]
-    starts = [which * 2048 + lax.rem(own[which] + d, 4) * 512 for which, d in plan]
-    over = [send(in_ref.at[rows_at(other + start, 512)], core_buf.at[rows_at(start, 512)], partner) for start in starts]
-    first = {}
-    for (which, d), start, copy in zip(plan, starts, over):
-        copy.wait_recv()
-        if d:
-
-            @pl.loop(0, 2)
-            def _(step):
-                here = rows_at(start + step * 256, 256)
-                value = in_ref[rows_at(mine + start + step * 256, 256), :].astype(F32)
-                half[here, :] = (value + core_buf[here, :].astype(F32)).astype(BF16)
-
-            first[which, d] = send(
-                half.at[rows_at(start, 512)], buf1.at[which, d - 1], (xs, ys)[which][d - 1]
-            )
-    second = {}
-    for which in range(2):
-        for d in range(1, 4):
-            first[which, d].wait_recv()
-        for d in (1, 2, 3, 0):
-            piece = lax.rem(own[1 - which] + d, 4) * 128
-            here = rows_at(piece, 128)
-            start = which * 2048 + own[which] * 512 + piece
-            total = in_ref[rows_at(mine + start, 128), :].astype(F32) + core_buf[rows_at(start, 128), :].astype(F32)
-            for e in range(3):
-                total += buf1[which, e, here, :].astype(F32)
-            if d:
-                sum1[which, here, :] = total.astype(BF16)
-                second[which, d] = send(sum1.at[which, here], buf2.at[which, d - 1], (ys, xs)[which][d - 1])
-            else:
-                sum2[:, which] = total.reshape(8, 16, 128)
-    for which in range(2):
-        for d in range(1, 4):
-            second[which, d].wait_recv()
-        sum2[:, which] = sum2[:, which] + (
-            buf2[which, 0].astype(F32) + buf2[which, 1].astype(F32) + buf2[which, 2].astype(F32)
-        ).reshape(8, 16, 128)
-    third = [send(sum2.at[lax.rem(z + d, 8)], buf3.at[d - 1], zs[d - 1]) for d in range(1, 8)]
-    for copy in third:
-        copy.wait_recv()
-    total = sum2[z]
-    for d in range(7):
-        total += buf3[d]
-    base = (mine + x * 512 + y * 128, mine + 2048 + y * 512 + x * 128)
-    back = {}
-    for which in range(2):
-        block = out_ref.at[rows_at(base[which] + z * 16, 16)]
-        out_ref[rows_at(base[which] + z * 16, 16), :] = total[which].astype(BF16)
-        for d in range(1, 8):
-            back[which, d] = send(block, block, zs[d - 1])
-    wide = {}
-    for which in range(2):
-        for d in range(1, 8):
-            back[which, d].wait_recv()
-        block = out_ref.at[rows_at(base[which], 128)]
-        for d in range(1, 4):
-            wide[which, d] = send(block, block, (ys, xs)[which][d - 1])
-    last, across = {}, []
-    for which in range(2):
-        for d in range(1, 4):
-            wide[which, d].wait_recv()
-        block = out_ref.at[rows_at(mine + which * 2048 + own[which] * 512, 512)]
-        for d in range(1, 4):
-            last[which, d] = send(block, block, (xs, ys)[which][d - 1])
-        across.append(send(block, block, partner))
-    for d in range(1, 4):
-        for which in range(2):
-            last[which, d].wait_recv()
-            block = out_ref.at[rows_at(mine + which * 2048 + lax.rem(own[which] + 4 - d, 4) * 512, 512)]
-            across.append(send(block, block, partner))
-    for copy in across:
-        copy.wait_recv()
-    for copy in started:
-        copy.wait_send()
-
-
-def reduce_all(values):
-    return pl.pallas_call(
-        reduce_kernel,
-        out_shape=jax.ShapeDtypeStruct((8192, 128), BF16),
-        in_specs=[pl.BlockSpec(memory_space=pltpu.VMEM)],
-        out_specs=pl.BlockSpec(memory_space=pltpu.VMEM),
-        scratch_shapes=[
-            pltpu.VMEM((4096, 128), BF16),
-            pltpu.VMEM((4096, 128), BF16),
-            pltpu.VMEM((2, 3, 512, 128), BF16),
-            pltpu.VMEM((2, 512, 128), BF16),
-            pltpu.VMEM((2, 3, 128, 128), BF16),
-            pltpu.VMEM((8, 2, 16, 128), F32),
-            pltpu.VMEM((7, 2, 16, 128), F32),
-            pltpu.SemaphoreType.DMA((61,)),
-            pltpu.SemaphoreType.DMA((61,)),
-        ],
-        compiler_params=pltpu.CompilerParams(
-            collective_id=0, has_side_effects=True, vmem_limit_bytes=VMEM_LIMIT
-        ),
-        name="reduce_all",
-    )(values)
-
-
-def pair_sum_kernel(in_ref, out_ref, got, send_sem, recv_sem):
-    x, y, z, core = place()
-    partner = peer(x, y, z, 1 - core)
-    barrier = pltpu.get_barrier_semaphore()
-    pl.semaphore_signal(barrier, inc=1, device_id=partner, device_id_type=MESH)
-    pl.semaphore_wait(barrier, 1)
-    copies = []
-    for part in range(4):
-        here = pl.ds(part * 1024, 1024)
-        copy = pltpu.make_async_remote_copy(
-            src_ref=in_ref.at[here], dst_ref=got.at[here], send_sem=send_sem.at[part],
-            recv_sem=recv_sem.at[part], device_id=partner, device_id_type=MESH,
-        )
-        copy.start()
-        copies.append(copy)
-    for part in range(4):
-        here = pl.ds(part * 1024, 1024)
-        copies[part].wait()
-        out_ref[here, :] = in_ref[here, :].astype(F32) + got[here, :].astype(F32)
-
-
-def pair_sum(values):
-    return pl.pallas_call(
-        pair_sum_kernel,
-        out_shape=jax.ShapeDtypeStruct((4096, 128), F32),
-        in_specs=[pl.BlockSpec(memory_space=pltpu.VMEM)],
-        out_specs=pl.BlockSpec(memory_space=pltpu.VMEM),
-        scratch_shapes=[
-            pltpu.VMEM((4096, 128), BF16),
-            pltpu.SemaphoreType.DMA((4,)),
-            pltpu.SemaphoreType.DMA((4,)),
-        ],
-        compiler_params=pltpu.CompilerParams(
-            collective_id=1, has_side_effects=True, vmem_limit_bytes=VMEM_LIMIT
-        ),
-        name="pair_sum",
-    )(values)
 
 
 def params():
@@ -217,7 +49,6 @@
     dx = (lax.bitwise_and(lax.shift_right_logical(owner, 3), 3) - x + 4) & 3
     dy = (lax.shift_right_logical(owner, 5) - y + 4) & 3
     relative = dz * 16 + dy * 4 + dx
-    owner = owner.astype(F32)
     lane = iota((256, 128), 1)
     named = jnp.zeros((256, 128), F32)
     wanted = jnp.zeros((256, 128), F32)
@@ -230,12 +61,17 @@
     back_x = (4 - dx) & 3
     block = ((((4 - dy) & 3) * 4 + back_x) * 8 + ((8 - dz) & 7)) * 64
     block, late = block.astype(F32), (4 * back_x).astype(F32)
+    base = ((dy * 8 + dz) * 208).astype(F32)
+    ahead = dx.astype(F32)
     slots = jnp.zeros((256, 128), F32)
     places = jnp.zeros((256, 128), F32)
     for f in range(13):
         here = relative[:, f : f + 1] == lane
         mine = jnp.sum(jnp.where(here, count, 0.0), axis=1, keepdims=True)
-        slots = jnp.where(lane == f, owner[:, f : f + 1] * STRIDE + mine, slots)
+        past = mine - float(EARLY)
+        over = ahead[:, f : f + 1]
+        spot = jnp.where(past < 0.0, over * float(EARLY) + mine, 4.0 * EARLY + 4.0 * over + past)
+        slots = jnp.where(lane == f, base[:, f : f + 1] + spot, slots)
         inside = jnp.where(mine < float(EARLY), mine, mine + late[:, f : f + 1])
         places = jnp.where(lane == f, block[:, f : f + 1] + inside, places)
     slot_ref[...] = slots.T[0:16, :].astype(jnp.int32)
@@ -245,8 +81,13 @@
     table[...] = jnp.zeros((128, 128), F32)
 
     for p in range(CAP):
-        chosen = jnp.where(rank[...] == float(p), rows[...], 0.0)
-        table[p : p + 1, :] = jnp.sum(chosen, axis=0, keepdims=True)
+        chosen = jnp.sum(jnp.where(rank[...] == float(p), rows[...], 0.0), axis=0, keepdims=True)
+        if p < EARLY:
+            table[p : p + 1, :] = chosen
+        else:
+            for e in range(4):
+                at = EARLY + e * 4 + p - EARLY
+                table[at : at + 1, :] = jnp.where((iota((1, 128), 1) & 3) == e, chosen, -1.0)
 
     query_ref[...] = table[...].T.astype(jnp.int32).reshape(8, 16, 128)
 
@@ -265,11 +106,6 @@
     )(cold_owner, cold_row)
 
 
-def source_of(r, x, y, z):
-    dz, dx, dy = lax.rem(r, 8), lax.rem(lax.div(r, 8), 4), lax.div(r, 32)
-    return lax.rem(y - dy + 4, 4) * 32 + lax.rem(x - dx + 4, 4) * 8 + lax.rem(z - dz + 8, 8)
-
-
 def widen(wide, ref, rows):
     @pl.loop(0, rows // 256)
     def _(step):
@@ -278,9 +114,9 @@
 
 
 def front_kernel(
-    query_ref, table_ref, index_ref, hot_table_ref, dense_ref, weight_ref, top_ref,
+    query_ref, table_far, index_far, hot_table_far, dense_far, weight_far, top_far,
     want_ref, got_ref, near_ref, bottom_ref, square_ref,
-    tall, middle, turned, wanted, wide, wide_hot, held, chosen, passing, send_sem, recv_sem, local_sem,
+    table_ref, index_ref, hot_table_ref, dense_ref, weight_ref, top_ref, tall, middle, turned, wanted, wide, wide_hot, held, chosen, passing, send_sem, recv_sem, local_sem,
 ):
     x, y, z, core = place()
     plane = [(dx, dy) for dy in range(4) for dx in range(4)]
@@ -289,7 +125,13 @@
     barrier = pltpu.get_barrier_semaphore()
     for other in zs + xys:
         pl.semaphore_signal(barrier, inc=1, device_id=other, device_id_type=MESH)
-    widen(wide, table_ref, 4096)
+    fetched = (
+        (table_far, table_ref), (index_far, index_ref), (hot_table_far, hot_table_ref),
+        (dense_far, dense_ref), (weight_far, weight_ref), (top_far, top_ref),
+    )
+    fetches = [pltpu.make_async_copy(src, dst, local_sem.at[1 + n]) for n, (src, dst) in enumerate(fetched)]
+    for fetch in fetches:
+        fetch.start()
     pl.semaphore_wait(barrier, len(zs) + len(xys))
 
     started = []
@@ -306,6 +148,8 @@
 
     copies = [send(query_ref.at[d], middle.at[d], zs[d - 1]) for d in range(1, 8)]
     middle[0] = query_ref[0]
+    fetches[0].wait()
+    widen(wide, table_ref, 4096)
     for copy in copies:
         copy.wait_recv()
     for d in range(8):
@@ -315,7 +159,7 @@
     want_ref[0] = turned[0]
     for copy in copies:
         copy.wait_recv()
-    copy = pltpu.make_async_copy(want_ref, wanted, local_sem)
+    copy = pltpu.make_async_copy(want_ref, wanted, local_sem.at[0])
     copy.start()
     copy.wait()
 
@@ -330,7 +174,7 @@
             for tile in range(13):
                 rows = []
                 for e in range(16):
-                    dx, p = (tile // 3, tile % 3 * 16 + e) if tile < 12 else (e // 4, EARLY + e % 4)
+                    dx, p = (tile // 3, tile % 3 * 16 + e) if tile < 12 else (e // 4, EARLY + (4 - e // 4) % 4 * 4 + e % 4)
                     k = (4 - dy) % 4 * 4 + (4 - dx) % 4
                     rows.append(wide[pl.ds(wanted[k, back, p], 1), :])
                 chosen[dy, d, tile * 16 : tile * 16 + 16, :] = jnp.concatenate(rows, axis=0).astype(BF16)
@@ -355,6 +199,8 @@
 
     collect(order[0])
     collect(order[1])
+    for fetch in fetches[1:]:
+        fetch.wait()
     widen(wide_hot, hot_table_ref, 4096)
     bottom = jnp.maximum(jnp.dot(dense_ref[...], weight_ref[...], preferred_element_type=F32), 0.0)
     bottom_ref[...] = bottom.astype(BF16)
@@ -408,9 +254,15 @@
             jax.ShapeDtypeStruct((256, 128), BF16),
             jax.ShapeDtypeStruct((896, 1024), BF16),
         ),
-        in_specs=[vmem, vmem, pl.BlockSpec(memory_space=pltpu.SMEM), vmem, vmem, vmem, vmem],
+        in_specs=[vmem] + [pl.BlockSpec(memory_space=pl.ANY)] * 6,
         out_specs=(vmem,) * 5,
         scratch_shapes=[
+            pltpu.VMEM((4096, 128), BF16),
+            pltpu.SMEM((13, 256), jnp.int32),
+            pltpu.VMEM((4096, 128), BF16),
+            pltpu.VMEM((256, 256), BF16),
+            pltpu.VMEM((256, 128), BF16),
+            pltpu.VMEM((479, 1024), BF16),
             pltpu.VMEM((512, 1024), BF16),
             pltpu.VMEM((8, 16, 128), jnp.int32),
             pltpu.VMEM((16, 8, 128), jnp.int32),
@@ -422,9 +274,9 @@
             pltpu.VMEM((4, 8, 208, 128), BF16),
             pltpu.SemaphoreType.DMA((80,)),
             pltpu.SemaphoreType.DMA((80,)),
-            pltpu.SemaphoreType.DMA,
+            pltpu.SemaphoreType.DMA((7,)),
         ],
-        compiler_params=pltpu.CompilerParams(collective_id=2, has_side_effects=True, vmem_limit_bytes=VMEM_LIMIT),
+        compiler_params=pltpu.CompilerParams(collective_id=2, has_side_effects=True, vmem_limit_bytes=60 * 1024 * 1024),
         name="front_part",
     )(query, table, hot_index, hot_table, dense, weight, top)
 
@@ -496,9 +348,9 @@
             grad_ref[...], weight_ref[here, :], (((1,), (1,)), ((), ())), preferred_element_type=F32
         )
 
-    @pl.loop(0, 7)
+    @pl.loop(0, 13)
     def _(step):
-        wide[pl.ds(pl.multiple_of(step * 1024, 1024), 1024), :] = jnp.zeros((1024, 128), F32)
+        wide[pl.ds(pl.multiple_of(step * 512, 512), 512), :] = jnp.zeros((512, 128), F32)
 
     @pl.loop(0, 32 // UNROLL)
     def _(step):
@@ -525,11 +377,10 @@
                     row = f * 8 + k
                     wide[pl.ds(slot_ref[f, g * 8 + k], 1), :] = terms[e, row : row + 1, :]
 
-    @pl.loop(0, 16)
+    @pl.loop(0, 26)
     def _(step):
-        for e in range(8):
-            d = step * 8 + e
-            sent_ref[d] = wide[pl.ds(pl.multiple_of(d * STRIDE, 8), CAP), :].astype(BF16)
+        here = pl.ds(pl.multiple_of(step * 256, 256), 256)
+        sent_ref[here, :] = wide[here, :].astype(BF16)
 
 
 def main_part(slot, places, got, near, bottom, weight0, weight, out_weight, clicks):
@@ -537,7 +388,7 @@
     return pl.pallas_call(
         main_kernel,
         out_shape=(
-            jax.ShapeDtypeStruct((128, CAP, 128), BF16),
+            jax.ShapeDtypeStruct((6656, 128), BF16),
             jax.ShapeDtypeStruct((13, 256, 128), F32),
             jax.ShapeDtypeStruct((256, 896), BF16),
             jax.ShapeDtypeStruct((256, 1024), BF16),
@@ -596,29 +447,171 @@
     out_ref[7936:8192, :] = jnp.zeros((256, 128), BF16)
 
 
-def hot_and_top(row, value, bottom, low, grad):
-    return pl.pallas_call(
-        hot_kernel,
-        out_shape=jax.ShapeDtypeStruct((8192, 128), BF16),
-        scratch_shapes=[pltpu.VMEM((3328, 256), BF16), pltpu.VMEM((480, 1024), F32)],
-        compiler_params=params(),
-        name="hot_and_top",
-    )(row, value, bottom, low, grad)
-
-
-def cold_kernel(want_ref, value_ref, out_ref, halves, joined):
-    x, y, z, _ = place()
-    pad = jnp.zeros((64 - CAP, 128), F32)
+def back_kernel(
+    sent_ref, want_ref, hot_row_ref, hot_value_ref, bottom_ref, low_ref, grad_ref,
+    out_ref, part_ref, other_ref,
+    in_ref, hot_halves, top, passing, got, halves, joined,
+    core_buf, half, buf1, sum1, buf2, sum2, buf3, send_sem, recv_sem,
+):
+    x, y, z, core = place()
+    plane = [(dx, dy) for dy in range(4) for dx in range(4)]
+    partner = peer(x, y, z, 1 - core)
+    zs = [peer(x, y, lax.rem(z + d, NZ), core) for d in range(1, NZ)]
+    xys = [peer(lax.rem(x + dx, NX), lax.rem(y + dy, NY), z, core) for dx, dy in plane[1:]]
+    xs = [xys[d - 1] for d in range(1, 4)]
+    ys = [xys[4 * d - 1] for d in range(1, 4)]
+    barrier = pltpu.get_barrier_semaphore()
+    everyone = [partner] + zs + xys
+    for other in everyone:
+        pl.semaphore_signal(barrier, inc=1, device_id=other, device_id_type=MESH)
+    pl.semaphore_wait(barrier, len(everyone))
+
+    started = []
+
+    def send(src, dst, device):
+        index = len(started)
+        copy = pltpu.make_async_remote_copy(
+            src_ref=src, dst_ref=dst, send_sem=send_sem.at[index], recv_sem=recv_sem.at[index],
+            device_id=device, device_id_type=MESH,
+        )
+        copy.start()
+        started.append(copy)
+        return copy
+
+    along, flat = {}, []
+
+    def set_out(dy):
+        for d in range(1, 8):
+            along[dy, d] = send(sent_ref.at[dy, d], passing.at[dy, d], zs[d - 1])
+        passing[dy, 0] = sent_ref[dy, 0]
+
+    def pass_on(dy):
+        for d in range(1, 8):
+            along[dy, d].wait_recv()
+        for dx in range(4):
+            early = passing.at[dy, :, pl.ds(dx * EARLY, EARLY)]
+            late = passing.at[dy, :, pl.ds(4 * EARLY, 16)]
+            k = dy * 4 + dx
+            if k:
+                flat.append(send(early, got.at[k, :, pl.ds(0, EARLY)], xys[k - 1]))
+                flat.append(send(late, got.at[k, :, pl.ds(EARLY, 16)], xys[k - 1]))
+            else:
+                got[0, :, 0:EARLY, :] = passing[0, :, 0:EARLY, :]
+                got[0, :, EARLY:64, :] = passing[0, :, 4 * EARLY : 4 * EARLY + 16, :]
+
+    set_out(2)
+    set_out(1)
+    hot_kernel(hot_row_ref, hot_value_ref, bottom_ref, low_ref, grad_ref, in_ref, hot_halves, top)
+
+    mine, other = core * 4096, (1 - core) * 4096
+    own = (x, y)
+    plan = [(which, d) for d in (1, 2, 3, 0) for which in (0, 1)]
+    starts = [which * 2048 + lax.rem(own[which] + d, 4) * 512 for which, d in plan]
+    over = [send(in_ref.at[rows_at(other + start, 512)], core_buf.at[rows_at(start, 512)], partner) for start in starts]
+    pass_on(2)
+    set_out(3)
+    first = {}
+    for (which, d), start, copy in zip(plan, starts, over):
+        copy.wait_recv()
+        if d:
+
+            @pl.loop(0, 2)
+            def _(step):
+                here = rows_at(start + step * 256, 256)
+                value = in_ref[rows_at(mine + start + step * 256, 256), :].astype(F32)
+                half[here, :] = (value + core_buf[here, :].astype(F32)).astype(BF16)
+
+            first[which, d] = send(
+                half.at[rows_at(start, 512)], buf1.at[which, d - 1], (xs, ys)[which][d - 1]
+            )
+    pass_on(1)
+    set_out(0)
+    second = {}
+    for which in range(2):
+        for d in range(1, 4):
+            first[which, d].wait_recv()
+        for d in (1, 2, 3, 0):
+            piece = lax.rem(own[1 - which] + d, 4) * 128
+            here = rows_at(piece, 128)
+            start = which * 2048 + own[which] * 512 + piece
+            total = in_ref[rows_at(mine + start, 128), :].astype(F32) + core_buf[rows_at(start, 128), :].astype(F32)
+            for e in range(3):
+                total += buf1[which, e, here, :].astype(F32)
+            if d:
+                sum1[which, here, :] = total.astype(BF16)
+                second[which, d] = send(sum1.at[which, here], buf2.at[which, d - 1], (ys, xs)[which][d - 1])
+            else:
+                sum2[:, which] = total.reshape(8, 16, 128)
+    for which in range(2):
+        for d in range(1, 4):
+            second[which, d].wait_recv()
+        sum2[:, which] = sum2[:, which] + (
+            buf2[which, 0].astype(F32) + buf2[which, 1].astype(F32) + buf2[which, 2].astype(F32)
+        ).reshape(8, 16, 128)
+    third = [send(sum2.at[lax.rem(z + d, 8)], buf3.at[d - 1], zs[d - 1]) for d in range(1, 8)]
+    pass_on(3)
+    for copy in third:
+        copy.wait_recv()
+    total = sum2[z]
+    for d in range(7):
+        total += buf3[d]
+    base = (mine + x * 512 + y * 128, mine + 2048 + y * 512 + x * 128)
+    back = {}
+    for which in range(2):
+        block = out_ref.at[rows_at(base[which] + z * 16, 16)]
+        out_ref[rows_at(base[which] + z * 16, 16), :] = total[which].astype(BF16)
+        for d in range(1, 8):
+            back[which, d] = send(block, block, zs[d - 1])
+    pass_on(0)
+    wide = {}
+    for which in range(2):
+        for d in range(1, 8):
+            back[which, d].wait_recv()
+        block = out_ref.at[rows_at(base[which], 128)]
+        for d in range(1, 4):
+            wide[which, d] = send(block, block, (ys, xs)[which][d - 1])
+    for copy in flat:
+        copy.wait_recv()
+    cold_start(want_ref, got, halves, joined)
+    last, across = {}, []
+    for which in range(2):
+        for d in range(1, 4):
+            wide[which, d].wait_recv()
+        block = out_ref.at[rows_at(mine + which * 2048 + own[which] * 512, 512)]
+        for d in range(1, 4):
+            last[which, d] = send(block, block, (xs, ys)[which][d - 1])
+        across.append(send(block, block, partner))
+    for n in range(4):
+        cold_step(n, part_ref, halves, joined)
+        for low_row in (n * 512, n * 512 + 2048):
+            block = pl.ds(low_row, 512)
+            across.append(send(part_ref.at[block], other_ref.at[block], partner))
+        if n == 2:
+            for d in range(1, 4):
+                for which in range(2):
+                    last[which, d].wait_recv()
+                    block = out_ref.at[rows_at(mine + which * 2048 + lax.rem(own[which] + 4 - d, 4) * 512, 512)]
+                    across.append(send(block, block, partner))
+    for copy in across:
+        copy.wait_recv()
+    for copy in started:
+        copy.wait_send()
+
+
+def cold_start(want_ref, got, halves, joined):
     even, odd = want_ref[pl.ds(0, 64, stride=2), :], want_ref[pl.ds(1, 64, stride=2), :]
-    joined[...] = jnp.where(iota((64, 128), 1) < 64, even, pltpu.roll(odd, 64, 1)) & 2047
+    both = jnp.where(iota((64, 128), 1) < 64, even, pltpu.roll(odd, 64, 1))
+    joined[...] = jnp.where(both < 0, -1, both & 2047)
     columns = (want_ref[...] >> 11).astype(F32).T
     for r in range(128):
         high = columns[0:64, r : r + 1]
-        value = jnp.concatenate([value_ref[source_of(r, x, y, z)].astype(F32), pad], axis=0)
+        value = got[r // 8, r % 8].astype(F32)
         halves[r * 64 : r * 64 + 64, 0:128] = jnp.where(high == 0.0, value, 0.0).astype(BF16)
         halves[r * 64 : r * 64 + 64, 128:256] = jnp.where(high == 0.0, 0.0, value).astype(BF16)
 
-    @pl.loop(0, 8)
+
+def cold_step(part, out_ref, halves, joined):
+    @pl.loop(part * 2, part * 2 + 2)
     def _(m):
         start = pl.multiple_of(m * 256, 256)
         wanted = iota((256, 128), 0) + m * 256
@@ -635,29 +628,58 @@
         out_ref[pl.ds(start + 2048, 256), :] = total[:, 128:256].astype(BF16)
 
 
-def cold_sums(want, value):
+def back_part(sent, want, hot_row, hot_value, bottom, low, grad):
+    vmem = pl.BlockSpec(memory_space=pltpu.VMEM)
     return pl.pallas_call(
-        cold_kernel,
-        out_shape=jax.ShapeDtypeStruct((4096, 128), BF16),
-        scratch_shapes=[pltpu.VMEM((8192, 256), BF16), pltpu.VMEM((64, 128), jnp.int32)],
-        compiler_params=params(),
-        name="cold_sums",
-    )(want, value)
-
-
-def format_kernel(in_ref, hot_ref, top_ref):
+        back_kernel,
+        out_shape=(
+            jax.ShapeDtypeStruct((8192, 128), BF16),
+            jax.ShapeDtypeStruct((4096, 128), BF16),
+            jax.ShapeDtypeStruct((4096, 128), BF16),
+        ),
+        in_specs=[vmem] * 7,
+        out_specs=(vmem,) * 3,
+        scratch_shapes=[
+            pltpu.VMEM((8192, 128), BF16),
+            pltpu.VMEM((3328, 256), BF16),
+            pltpu.VMEM((480, 1024), F32),
+            pltpu.VMEM((4, 8, 208, 128), BF16),
+            pltpu.VMEM((16, 8, 64, 128), BF16),
+            pltpu.VMEM((8192, 256), BF16),
+            pltpu.VMEM((64, 128), jnp.int32),
+            pltpu.VMEM((4096, 128), BF16),
+            pltpu.VMEM((4096, 128), BF16),
+            pltpu.VMEM((2, 3, 512, 128), BF16),
+            pltpu.VMEM((2, 512, 128), BF16),
+            pltpu.VMEM((2, 3, 128, 128), BF16),
+            pltpu.VMEM((8, 2, 16, 128), F32),
+            pltpu.VMEM((7, 2, 16, 128), F32),
+            pltpu.SemaphoreType.DMA((127,)),
+            pltpu.SemaphoreType.DMA((127,)),
+        ],
+        compiler_params=pltpu.CompilerParams(collective_id=0, has_side_effects=True, vmem_limit_bytes=VMEM_LIMIT),
+        name="back_part",
+    )(sent, want, hot_row, hot_value, bottom, low, grad)
+
+
+def format_kernel(in_ref, part_ref, other_ref, hot_ref, cold_ref, top_ref):
     hot_ref[...] = in_ref[0:4096, :].astype(F32)
+    cold_ref[...] = part_ref[...].astype(F32) + other_ref[...].astype(F32)
     for n in range(8):
         top_ref[:, n * 128 : n * 128 + 128] = in_ref[4096 + n * 480 : 4576 + n * 480, :].astype(F32)[0:479, :]
 
 
-def format_sums(values):
+def format_sums(values, part, other):
     return pl.pallas_call(
         format_kernel,
-        out_shape=(jax.ShapeDtypeStruct((4096, 128), F32), jax.ShapeDtypeStruct((479, 1024), F32)),
+        out_shape=(
+            jax.ShapeDtypeStruct((4096, 128), F32),
+            jax.ShapeDtypeStruct((4096, 128), F32),
+            jax.ShapeDtypeStruct((479, 1024), F32),
+        ),
         compiler_params=params(),
         name="format_sums",
-    )(values)
+    )(values, part, other)
 
 
 def body(
@@ -681,12 +703,10 @@
     outgoing, hot_terms, low, grad = main_part(
         slot, places, got.reshape(8192, 128), near, bottom, top_weight, weight, out_weight.reshape(1, 1024), clicks.reshape(1, 256)
     )
-    returned = lax.all_to_all(outgoing, "dp", split_axis=0, concat_axis=0, tiled=True)
-    sums = hot_and_top(hot_fields, hot_terms, bottom, low, grad)
-    hot_grad, top_grad = format_sums(reduce_all(sums))
-    local_cold = cold_sums(wanted, returned)
-    cold_grad = pair_sum(local_cold)
-    return (hot_grad, cold_grad, top_grad)
+    sums, part, other = back_part(
+        outgoing.reshape(4, 8, 208, 128), wanted, hot_fields, hot_terms, bottom, low, grad
+    )
+    return format_sums(sums, part, other)
 
 
 def solution(mesh):

time: 200 us -> 187 us (0.935)
  starting transfers between devices: 10.9 us -> 0 us
  local copies, waits for them, and re-layouts: 14 us -> 6.44 us
  Pallas kernels: 174 us -> 179 us
    all_to_all x1 -> x0, starting transfers between devices: 10.9 us -> none  [body(): lax.all_to_all(outgoing, 'dp', split_axis=0, concat_axis=0, tiled=True)]
    unnamed x39 -> x22, local copies, waits for them, and re-layouts: 13.3 us -> 5.67 us
    pallas_call x5 -> x2, Pallas kernels: 99.2 us -> 104 us  [the longest x1 82.8 us: back_part(): pl.pallas_call(back_kernel, out_shape=(jax.ShapeDtypeStruct((8192, 128),...]
  transfers between devices with their start and end apart: 1 -> 0, of which waited for: 0 -> 0; matrix products, arithmetic and copies ran while one was open for 0% -> 0% of each run, Pallas kernels for 33% -> 0%
where the time goes in v2:
time: 187 us; the launch traced here: 186 us
  Pallas kernels  179 us (96%)
  local copies, waits for them, and re-layouts  6.44 us (3%)
    pallas_call x1, Pallas kernels, back_part(): pl.pallas_call(back_kernel, out_shape=(jax.ShapeDtypeStruct((8192, 128),...  82.8 us
    pallas_call x1, Pallas kernels, front_part(): pl.pallas_call(front_kernel, out_shape=(jax.ShapeDtypeStruct((16, 8, 128)...  68 us
    pallas_call x1, Pallas kernels, main_part(): pl.pallas_call(main_kernel, out_shape=(jax.ShapeDtypeStruct((6656, 128),...  21.5 us
    unnamed x22, local copies, waits for them, and re-layouts  5.67 us
    pallas_call x1, Pallas kernels, build_requests(): pl.pallas_call(build_kernel, out_shape=(jax.ShapeDtypeStruct((8, 16, 128)...  4.11 us

profile of v2, /device:TPU:1, one launch (start us, length us, event | category | flops | bytes accessed | tf_op | source)
XLA Modules:
  0.0 186.4 jit_solution(15243574595176779750)
XLA Ops:
  0.6 0.0 copy-start
  0.6 0.8 reshape.22.out_weight_ref
  1.4 0.0 copy-start.8
  1.4 0.7 copy-done.8
  2.1 0.0 copy-start.9
  2.1 0.7 copy-done.9
  2.8 0.0 copy-start.10
  2.9 4.1 %build_requests.1 = (s32[8,16,128]{2,1,0:T(8,128)S(1)}, s32[16,256]{1,0:T(8,128)S(1)}, s32[16,256]{1,0:T(8,128)S(1)}) custom-call(s32[13,256]{1,0:T(8,128)S(1)} %bitcast.11, s32[13,256]{1,0:T(8,128)S(1)} %bitcast.12), custom_call_target="tpu_custom_call" | custom-call | tf_op jit(solution)/shard_map/build_requests/pallas_call | solution.py:96
  7.0 0.0 copy-start.7
  7.0 0.6 copy-done.7
  7.6 68.0 %front_part.1 = (s32[16,8,128]{2,1,0:T(8,128)}, bf16[16,8,64,128]{3,2,1,0:T(8,128)(2,1)}, bf16[32,112,128]{2,1,0:T(8,128)(2,1)}, bf16[256,128]{1,0:T(8,128)(2,1)}, bf16[896,1024]{1,0:T(8,128)(2,1)}) custom-call(s32[8,16,128]{2,1,0:T(8,128)} %copy-done.7, bf16[4096,128]{1,0:T(8,128)(2,1)} %table_far.1, s32[13,256]{1,0:T(8,128)} %bitcast.9, ...), custom_call_target="tpu_custom_call" | custom-call | tf_op jit(solution)/shard_map/front_part/pallas_call | solution.py:248
  75.6 0.0 copy-done
  75.6 0.0 copy-done.10
  75.6 0.0 copy-start.2
  75.6 1.2 copy-done.2
  76.8 0.8 copy-done.3
  77.6 21.5 %main_part.1 = (bf16[6656,128]{1,0:T(8,128)(2,1)S(1)}, f32[13,256,128]{2,1,0:T(8,128)}, bf16[256,896]{1,0:T(8,128)(2,1)S(1)}, bf16[256,1024]{1,0:T(8,128)(2,1)S(1)}) custom-call(s32[16,256]{1,0:T(8,128)S(1)} %get-tuple-element.18.slot_ref, s32[16,256]{1,0:T(8,128)S(1)} %get-tuple-element.19.place_ref, bf16[8192,128]{1,0:T(8,128)(2,1)} %bitcast.14, ...), custom_call_target="tpu_custom_call" | custom-call | tf_op jit(solution)/shard_map/main_part/pallas_call | solution.py:388
  99.1 0.0 copy-done.4
  99.1 0.0 copy-done.5
  99.1 0.0 copy-done.6
  99.1 82.8 %back_part.1 = (bf16[8192,128]{1,0:T(8,128)(2,1)}, bf16[4096,128]{1,0:T(8,128)(2,1)S(1)}, bf16[4096,128]{1,0:T(8,128)(2,1)S(1)}) custom-call(bf16[4,8,208,128]{3,2,1,0:T(8,128)(2,1)S(1)} %bitcast.7, s32[128,128]{1,0:T(8,128)S(1)} %bitcast.8, s32[13,256]{1,0:T(8,128)S(1)} %bitcast.10, f32[13,256,128]{2,1,0:T(8,128)} %get-tuple-element.27.hot_value_ref, ...), custom_call_target="tpu_custom_call" | custom-call | tf_op jit(solution)/shard_map/back_part/pallas_call | solution.py:633
  181.9 0.0 copy-start.1
  181.9 1.6 copy-done.1
  183.5 3.0 %format_sums.1 = (f32[4096,128]{1,0:T(8,128)}, f32[4096,128]{1,0:T(8,128)}, f32[479,1024]{1,0:T(8,128)}) custom-call(bf16[8192,128]{1,0:T(8,128)(2,1)S(1)} %copy-done.1, bf16[4096,128]{1,0:T(8,128)(2,1)S(1)} %get-tuple-element.31.part_ref, bf16[4096,128]{1,0:T(8,128)(2,1)S(1)} %get-tuple-element.32.other_ref), custom_call_target="tpu_custom_call" | custom-call | tf_op jit(solution)/shard_map/format_sums/pallas_call | solution.py:673
  (4 shorter events, 0.0 us)
Async XLA Ops:
  0.6 74.9 %copy-start = (bf16[479,1024]{1,0:T(8,128)(2,1)S(1)}, bf16[479,1024]{1,0:T(8,128)(2,1)}, u32[]{:S(2)}) copy-start(bf16[479,1024]{1,0:T(8,128)(2,1)} %weight0_ref.1) | copy-start | bytes 2942980
  1.4 0.7 copy-start.8
  2.1 0.7 copy-start.9
  2.8 72.7 %copy-start.10 = (s32[256]{0:T(256)S(1)}, s32[256]{0:T(256)}, u32[]{:S(2)}) copy-start(s32[256]{0:T(256)} %param.19) | copy-start | bytes 3076
  7.0 0.6 copy-start.7
  75.6 1.2 copy-start.2
  76.8 0.8 copy-start.3
  77.6 21.5 %copy-start.4 = (bf16[256,128]{1,0:T(8,128)(2,1)S(1)}, bf16[256,128]{1,0:T(8,128)(2,1)}, u32[]{:S(2)}) copy-start(bf16[256,128]{1,0:T(8,128)(2,1)} %get-tuple-element.23.bottom_ref) | copy-start | bytes 196612
  77.6 21.5 %copy-start.5 = (s32[16,8,128]{2,1,0:T(8,128)S(1)}, s32[16,8,128]{2,1,0:T(8,128)}, u32[]{:S(2)}) copy-start(s32[16,8,128]{2,1,0:T(8,128)} %get-tuple-element.26) | copy-start | bytes 196612
  77.6 21.5 %copy-start.6 = (s32[256,13]{0,1:T(8,128)S(1)}, s32[256,13]{0,1:T(8,128)}, u32[]{:S(2)}) copy-start(s32[256,13]{0,1:T(8,128)} %param.16) | copy-start | bytes 39940
  181.9 1.6 copy-start.1

commit v3 on v2

--- a/solution.py
+++ b/solution.py
@@ -197,8 +197,8 @@
                 got_ref[0, :, 0:EARLY, :] = passing[0, :, 0:EARLY, :]
                 got_ref[0, :, EARLY:64, :] = passing[0, :, 4 * EARLY : 4 * EARLY + 16, :]
 
-    collect(order[0])
-    collect(order[1])
+    for dy in order:
+        collect(dy)
     for fetch in fetches[1:]:
         fetch.wait()
     widen(wide_hot, hot_table_ref, 4096)
@@ -217,9 +217,7 @@
             near_ref[g, 8 + f * 8 : 24 + f * 8, :] = jnp.concatenate(rows, axis=0).astype(BF16)
 
     pass_on(order[0])
-    collect(order[2])
     pass_on(order[1])
-    collect(order[3])
     tall[464:512, :] = jnp.zeros((48, 1024), BF16)
     tall[0:479, :] = top_ref[...]
 

time: 187 us -> 189 us (1.011)
  Pallas kernels: 179 us -> 182 us
where the time goes in v3:
time: 189 us
  Pallas kernels  182 us (96%)
  local copies, waits for them, and re-layouts  6.44 us (3%)
    pallas_call x1, Pallas kernels, back_part(): pl.pallas_call(back_kernel, out_shape=(jax.ShapeDtypeStruct((8192, 128),...  84.3 us
    pallas_call x1, Pallas kernels, front_part(): pl.pallas_call(front_kernel, out_shape=(jax.ShapeDtypeStruct((16, 8, 128)...  68.7 us
    pallas_call x1, Pallas kernels, main_part(): pl.pallas_call(main_kernel, out_shape=(jax.ShapeDtypeStruct((6656, 128),...  21.5 us
    unnamed x22, local copies, waits for them, and re-layouts  5.67 us
    pallas_call x1, Pallas kernels, build_requests(): pl.pallas_call(build_kernel, out_shape=(jax.ShapeDtypeStruct((8, 16, 128)...  4.11 us

profile of v3, /device:TPU:1, one launch (start us, length us, event | category | flops | bytes accessed | tf_op | source)
XLA Modules:
  0.0 188.7 jit_solution(7379137008047213283)
XLA Ops:
  0.6 0.0 copy-start
  0.6 0.8 reshape.22.out_weight_ref
  1.4 0.0 copy-start.8
  1.4 0.7 copy-done.8
  2.1 0.0 copy-start.9
  2.1 0.7 copy-done.9
  2.8 0.0 copy-start.10
  2.9 4.1 %build_requests.1 = (s32[8,16,128]{2,1,0:T(8,128)S(1)}, s32[16,256]{1,0:T(8,128)S(1)}, s32[16,256]{1,0:T(8,128)S(1)}) custom-call(s32[13,256]{1,0:T(8,128)S(1)} %bitcast.11, s32[13,256]{1,0:T(8,128)S(1)} %bitcast.12), custom_call_target="tpu_custom_call" | custom-call | tf_op jit(solution)/shard_map/build_requests/pallas_call | solution.py:96
  7.0 0.0 copy-start.7
  7.0 0.6 copy-done.7
  7.6 68.7 %front_part.1 = (s32[16,8,128]{2,1,0:T(8,128)}, bf16[16,8,64,128]{3,2,1,0:T(8,128)(2,1)}, bf16[32,112,128]{2,1,0:T(8,128)(2,1)}, bf16[256,128]{1,0:T(8,128)(2,1)}, bf16[896,1024]{1,0:T(8,128)(2,1)}) custom-call(s32[8,16,128]{2,1,0:T(8,128)} %copy-done.7, bf16[4096,128]{1,0:T(8,128)(2,1)} %table_far.1, s32[13,256]{1,0:T(8,128)} %bitcast.9, ...), custom_call_target="tpu_custom_call" | custom-call | tf_op jit(solution)/shard_map/front_part/pallas_call | solution.py:246
  76.3 0.0 copy-done
  76.3 0.0 copy-done.10
  76.3 0.0 copy-start.2
  76.3 1.2 copy-done.2
  77.5 0.8 copy-done.3
  78.3 21.5 %main_part.1 = (bf16[6656,128]{1,0:T(8,128)(2,1)S(1)}, f32[13,256,128]{2,1,0:T(8,128)}, bf16[256,896]{1,0:T(8,128)(2,1)S(1)}, bf16[256,1024]{1,0:T(8,128)(2,1)S(1)}) custom-call(s32[16,256]{1,0:T(8,128)S(1)} %get-tuple-element.18.slot_ref, s32[16,256]{1,0:T(8,128)S(1)} %get-tuple-element.19.place_ref, bf16[8192,128]{1,0:T(8,128)(2,1)} %bitcast.14, ...), custom_call_target="tpu_custom_call" | custom-call | tf_op jit(solution)/shard_map/main_part/pallas_call | solution.py:386
  99.8 0.0 copy-done.4
  99.8 0.0 copy-done.5
  99.8 0.0 copy-done.6
  99.8 84.3 %back_part.1 = (bf16[8192,128]{1,0:T(8,128)(2,1)}, bf16[4096,128]{1,0:T(8,128)(2,1)S(1)}, bf16[4096,128]{1,0:T(8,128)(2,1)S(1)}) custom-call(bf16[4,8,208,128]{3,2,1,0:T(8,128)(2,1)S(1)} %bitcast.7, s32[128,128]{1,0:T(8,128)S(1)} %bitcast.8, s32[13,256]{1,0:T(8,128)S(1)} %bitcast.10, f32[13,256,128]{2,1,0:T(8,128)} %get-tuple-element.27.hot_value_ref, ...), custom_call_target="tpu_custom_call" | custom-call | tf_op jit(solution)/shard_map/back_part/pallas_call | solution.py:631
  184.1 0.0 copy-start.1
  184.1 1.6 copy-done.1
  185.7 3.0 %format_sums.1 = (f32[4096,128]{1,0:T(8,128)}, f32[4096,128]{1,0:T(8,128)}, f32[479,1024]{1,0:T(8,128)}) custom-call(bf16[8192,128]{1,0:T(8,128)(2,1)S(1)} %copy-done.1, bf16[4096,128]{1,0:T(8,128)(2,1)S(1)} %get-tuple-element.31.part_ref, bf16[4096,128]{1,0:T(8,128)(2,1)S(1)} %get-tuple-element.32.other_ref), custom_call_target="tpu_custom_call" | custom-call | tf_op jit(solution)/shard_map/format_sums/pallas_call | solution.py:671
  (4 shorter events, 0.0 us)
Async XLA Ops:
  0.6 75.7 %copy-start = (bf16[479,1024]{1,0:T(8,128)(2,1)S(1)}, bf16[479,1024]{1,0:T(8,128)(2,1)}, u32[]{:S(2)}) copy-start(bf16[479,1024]{1,0:T(8,128)(2,1)} %weight0_ref.1) | copy-start | bytes 2942980
  1.4 0.7 copy-start.8
  2.1 0.7 copy-start.9
  2.8 73.4 %copy-start.10 = (s32[256]{0:T(256)S(1)}, s32[256]{0:T(256)}, u32[]{:S(2)}) copy-start(s32[256]{0:T(256)} %param.19) | copy-start | bytes 3076
  7.0 0.6 copy-start.7
  76.3 1.2 copy-start.2
  77.5 0.8 copy-start.3
  78.3 21.5 %copy-start.4 = (bf16[256,128]{1,0:T(8,128)(2,1)S(1)}, bf16[256,128]{1,0:T(8,128)(2,1)}, u32[]{:S(2)}) copy-start(bf16[256,128]{1,0:T(8,128)(2,1)} %get-tuple-element.23.bottom_ref) | copy-start | bytes 196612
  78.3 21.5 %copy-start.5 = (s32[16,8,128]{2,1,0:T(8,128)S(1)}, s32[16,8,128]{2,1,0:T(8,128)}, u32[]{:S(2)}) copy-start(s32[16,8,128]{2,1,0:T(8,128)} %get-tuple-element.26) | copy-start | bytes 196612
  78.3 21.5 %copy-start.6 = (s32[256,13]{0,1:T(8,128)S(1)}, s32[256,13]{0,1:T(8,128)}, u32[]{:S(2)}) copy-start(s32[256,13]{0,1:T(8,128)} %param.16) | copy-start | bytes 39940
  184.1 1.6 copy-start.1
